TPU v7x, 128 devices: a whole 4x4x4 slice. The times are simulated.
128 devices in a mesh: kvh: 4 (over x), seq: 32 (over y, z, core).
Axes of the slice: x: 4, y: 4, z: 4, core: 2. Of those that a mesh axis runs over, the one named last changes fastest.
Arguments:
- queries: bfloat16 [8, 128, 128], P(None, 'kvh'), may hold values from -150 to 150
- key_cache: bfloat16 [8, 8, 4096, 128], P(None, 'kvh', 'seq'), may hold values from -6 to 6
- value_cache: bfloat16 [8, 8, 4096, 128], P(None, 'kvh', 'seq'), may hold values from -6 to 6
- new_keys: bfloat16 [8, 8, 128], P(None, 'kvh'), may hold values from -5 to 5
- new_values: bfloat16 [8, 8, 128], P(None, 'kvh'), may hold values from -6 to 6
- block_fill: int32 [8, 32], P(None, 'seq'), may hold values from 0 to 127, as said below
- new_block: int32 [8], replicated, may hold values from 0 to 31, as said below
- residual: float32 [8, 16384], P(None, ('kvh', 'seq')), may hold values from -5 to 5
- norm_gain: float32 [16384], P(('kvh', 'seq')), may hold values from 0.1 to 1.9
- out_weight: bfloat16 [16384, 16384], P(None, ('kvh', 'seq')), may hold values from -0.046875 to 0.046875
- gate_weight: bfloat16 [26624, 16384], P(('kvh', 'seq')), may hold values from -0.046875 to 0.046875
- up_weight: bfloat16 [26624, 16384], P(('kvh', 'seq')), may hold values from -0.046875 to 0.046875
- down_weight: bfloat16 [26624, 16384], P(('kvh', 'seq')), may hold values from -0.0390625 to 0.0390625
Outputs:
- layer_out: bfloat16 [8, 16384], P(None, ('kvh', 'seq'))
- keys_out: bfloat16 [8, 8, 4096, 128], P(None, 'kvh', 'seq')
- values_out: bfloat16 [8, 8, 4096, 128], P(None, 'kvh', 'seq')
Inputs may be any that keep to these rules, and one draw needn't show every extreme that they name: `block_fill`: the new row of a request goes to the row of its block just after the rows in use. `new_block`: the first min(8, 32) requests send their new rows to different blocks.
All inputs are finite; a program needn't handle non-finite values.
Results may differ from a plain program's by a relative error of at most 0.0075.
Values may be sent and summed in bfloat16 or wider, within the bound.
No kernel may reach another device: no remote copies, remote signals or barrier semaphores. Data moves between devices by JAX's collectives and lax.ppermute only.
A program may use at most 128 MiB of HBM per device.

v0:
```python
import jax
import jax.numpy as jnp
from jax import lax
from jax.sharding import PartitionSpec as P

D = 16384


def merged(value, axis, join):
    pieces = jax.tree.map(lambda part: lax.all_gather(part, axis), value)
    head = jax.tree.map(lambda part: part[0], pieces)
    tail = jax.tree.map(lambda part: part[1:], pieces)
    running, _ = lax.scan(lambda running, share: (join(running, share), None), head, tail)
    return running


def combine_partials(first, second):
    top_one, total_one, summed_one = first
    top_two, total_two, summed_two = second
    top = jnp.maximum(top_one, top_two)
    weight_one = jnp.exp(top_one - top)
    weight_two = jnp.exp(top_two - top)
    total = total_one * weight_one + total_two * weight_two
    summed = summed_one * weight_one[..., None] + summed_two * weight_two[..., None]
    return (top, total, summed)


def project_rows(normed, weight):
    return lax.dot_general(
        normed, weight, (((1,), (1,)), ((), ())), preferred_element_type=jnp.float32
    )


def body(
    queries,
    key_cache,
    value_cache,
    new_keys,
    new_values,
    block_fill,
    new_block,
    residual,
    norm_gain,
    out_weight,
    gate_weight,
    up_weight,
    down_weight,
):
    batch, heads_local, head_dim = queries.shape
    kv_local = key_cache.shape[1]
    group = heads_local // kv_local
    rows = key_cache.shape[2]
    block = lax.axis_index("seq")
    slots = jnp.arange(rows, dtype=jnp.int32)
    fresh = (slots[None, :] == block_fill) & (new_block[:, None] == block)
    live = (slots[None, :] < block_fill) | fresh
    keys_out = jnp.where(fresh[:, None, :, None], new_keys[:, :, None, :], key_cache)
    values_out = jnp.where(fresh[:, None, :, None], new_values[:, :, None, :], value_cache)
    grouped = queries.reshape(batch, kv_local, group, head_dim)
    scores = jnp.einsum(
        "bkgd,bktd->bkgt", grouped, keys_out, preferred_element_type=jnp.float32
    ) * head_dim ** (-0.5)
    mask = live[:, None, None, :]
    top = jnp.max(jnp.where(mask, scores, -1e30), axis=-1)
    weights = jnp.where(
        mask, jnp.exp(jnp.where(mask, scores, top[..., None]) - top[..., None]), 0.0
    )
    total = jnp.sum(weights, axis=-1)
    summed = jnp.einsum(
        "bkgt,bktd->bkgd", weights, values_out.astype(jnp.float32), precision=lax.Precision.HIGHEST
    )
    top = top.reshape(batch, heads_local)
    total = total.reshape(batch, heads_local)
    summed = summed.reshape(batch, heads_local, head_dim)
    top, total, summed = merged((top, total, summed), "seq", combine_partials)
    heads = (summed / total[..., None]).astype(jnp.bfloat16)
    every = lax.all_gather(heads, "kvh", axis=1, tiled=True)
    flat = every.reshape(batch, -1)
    mixed = residual + jnp.dot(flat, out_weight, preferred_element_type=jnp.float32)
    square = lax.psum(jnp.sum(mixed * mixed, axis=1), ("kvh", "seq"))
    factor_norm = lax.rsqrt(square / D + 1e-05)
    normed_share = (mixed * factor_norm[:, None] * norm_gain[None, :]).astype(jnp.bfloat16)
    normed = lax.all_gather(normed_share, ("kvh", "seq"), axis=1, tiled=True)
    gate = project_rows(normed, gate_weight)
    up_sum = project_rows(normed, up_weight)
    hidden = (jax.nn.silu(gate) * up_sum).astype(jnp.bfloat16)
    partial_down = jnp.dot(hidden, down_weight, preferred_element_type=jnp.float32)
    down_share = lax.psum_scatter(partial_down, ("kvh", "seq"), scatter_dimension=1, tiled=True)
    layer_out = (mixed + down_share).astype(jnp.bfloat16)
    return (layer_out, keys_out, values_out)


def solution(mesh):
    placed = (
        P(None, "kvh", None),
        P(None, "kvh", "seq", None),
        P(None, "kvh", "seq", None),
        P(None, "kvh", None),
        P(None, "kvh", None),
        P(None, "seq"),
        P(),
        P(None, ("kvh", "seq")),
        P(("kvh", "seq")),
        P(None, ("kvh", "seq")),
        P(("kvh", "seq"), None),
        P(("kvh", "seq"), None),
        P(("kvh", "seq"), None),
    )
    return jax.shard_map(
        body,
        mesh=mesh,
        in_specs=placed,
        out_specs=(
            P(None, ("kvh", "seq")),
            P(None, "kvh", "seq", None),
            P(None, "kvh", "seq", None),
        ),
        check_vma=False,
    )
```

profile of v0, /device:TPU:1, one launch (start us, length us, event | category | flops | bytes accessed | tf_op | source)
XLA Modules:
  0.0 867.1 jit_solution(6854087284841628084)
XLA Ops:
  7.2 0.0 copy-start
  7.2 0.0 all-gather.2.cloned.1.call-start
  7.2 0.7 broadcast_compare_fusion
  7.9 0.7 fusion.18
  8.6 1.4 broadcast_select_fusion
  10.0 0.0 copy-start.1
  10.1 0.0 copy-start.2
  10.1 0.0 copy-start.3
  10.1 0.5 select_reduce_fusion
  10.6 1.2 fusion.7
  11.8 0.0 all-gather.2.cloned.1.call-update
  11.8 0.0 reduce-scatter.2.cloned.1.call-start
  11.9 0.1 all_gather_reshape.9
  12.0 0.2 fusion.8
  12.2 0.1 all_gather_reshape.10
  12.3 27.4 %all_gather.16 = f32[32,8,32]{2,1,0:T(8,128)S(1)} all-gather(f32[1,8,32]{2,1,0:T(8,128)S(1)} %all_gather_reshape.10), channel_id=1, replica_groups=mesh['kvh'=4,'seq'=32] {'seq'}, dimensions={0}, use_global_device_ids=true | all-gather | bytes 33792 | tf_op jit(solution)/shard_map/all_gather | solution.py:10
  39.7 24.1 %all_gather.15 = f32[32,8,32]{2,1,0:T(8,128)S(1)} all-gather(f32[1,8,32]{2,1,0:T(8,128)S(1)} %all_gather_reshape.9), channel_id=1, replica_groups=mesh['kvh'=4,'seq'=32] {'seq'}, dimensions={0}, use_global_device_ids=true | all-gather | bytes 33792 | tf_op jit(solution)/shard_map/all_gather | solution.py:10
  63.8 0.0 copy-start.4
  63.8 0.0 all-gather.2.cloned.1.call-done
  63.8 4.8 slice.29
  68.6 0.9 slice_bitcast_fusion
  69.5 34.6 %while.14 = (s32[]{:T(128)}, f32[8,32]{1,0:T(8,128)S(1)}, f32[8,32]{1,0:T(8,128)S(1)}, f32[8,32,128]{2,1,0:T(8,128)S(1)}, f32[31,8,32]{2,1,0:T(8,128)S(1)}, /*in...) while((s32[]{:T(128)}, f32[8,32]{1,0:T(8,128)S(1)}, f32[8,32]{1,0:T(8,128)S(1)}, ...), condition=%wide.region_3.4_spmd, body=%wide.region_2.3_spmd.sunk | while | flops 99842 | bytes 403549 | solution.py:13
  69.5 1.1 fusion.36
  70.6 1.1 fusion.36
  71.7 1.1 fusion.36
  72.9 1.1 fusion.36
  74.0 1.1 fusion.36
  75.1 1.1 fusion.36
  76.2 1.1 fusion.36
  77.3 1.1 fusion.36
  78.4 1.1 fusion.36
  79.6 1.1 fusion.36
  80.7 1.1 fusion.36
  81.8 1.1 fusion.36
  82.9 1.1 fusion.36
  84.0 1.1 fusion.36
  85.1 1.1 fusion.36
  86.2 1.1 fusion.36
  87.4 1.1 fusion.36
  88.5 1.1 fusion.36
  89.6 1.1 fusion.36
  90.7 1.1 fusion.36
  91.8 1.1 fusion.36
  92.9 1.1 fusion.36
  94.1 1.1 fusion.36
  95.2 1.1 fusion.36
  96.3 1.1 fusion.36
  97.4 1.1 fusion.36
  98.5 1.1 fusion.36
  99.6 1.1 fusion.36
  100.8 1.1 fusion.36
  101.9 1.1 fusion.36
  103.0 1.1 fusion.36
  104.1 0.1 divide_convert_fusion
  104.2 10.2 %all_gather.18 = bf16[8,128,128]{2,1,0:T(8,128)(2,1)S(1)} all-gather(bf16[8,32,128]{2,1,0:T(8,128)(2,1)S(1)} %divide_convert_fusion), channel_id=1, replica_groups=mesh['kvh'=4,'seq'=32] {'kvh'}, dimensions={1}, use_global_device_ids=true | all-gather | bytes 327680 | tf_op jit(solution)/shard_map/all_gather | solution.py:77
  114.4 3.0 multiply_reduce_fusion
  117.4 64.2 %psum.7 = f32[8]{0:T(128)S(1)} all-reduce(f32[8]{0:T(128)S(1)} %get-tuple-element.67), channel_id=1, replica_groups=mesh['kvh'=4,'seq'=32] {'kvh','seq'}, use_global_device_ids=true, to_apply=%region_5.6 | all-reduce | flops 8 | bytes 64 | tf_op jit(solution)/shard_map/psum | solution.py:80
  181.7 0.1 multiply_convert_fusion
  181.7 33.6 %all_gather.19 = bf16[8,16384]{1,0:T(8,128)(2,1)S(1)} all-gather(bf16[8,128]{1,0:T(8,128)(2,1)S(1)} %multiply_convert_fusion), channel_id=1, replica_groups=mesh['kvh'=4,'seq'=32] {'kvh','seq'}, dimensions={1}, use_global_device_ids=true | all-gather | bytes 264192 | tf_op jit(solution)/shard_map/all_gather | solution.py:83
  215.3 4.8 fusion.23
  220.1 10.3 %fusion.4 = f32[8,16384]{1,0:T(8,128)} fusion(bf16[208,16384]{1,0:T(8,128)(2,1)} %param.27, bf16[8,16384]{1,0:T(8,128)(2,1)S(1)} %all_gather.19, bf16[208,16384]{1,0:T(8,128)(2,1)} %param.26, f32[8,208]{1,0:T(8,128)S(1)} %fusion.23), kind=kOutput, calls=%fused_computation.12 | convolution fusion | flops 109061888 | bytes 14424576 | tf_op jit(solution)/shard_map/dot_general | solution.py:87
  230.4 0.0 reduce-scatter.2.cloned.1.call-update
  230.4 628.6 %reduce-scatter.2.cloned.1.call-done = f32[8,128]{1,0:T(8,128)} async-done(((f32[8,16384]{1,0:T(8,128)}), f32[8,128]{1,0:T(8,128)}) %reduce-scatter.2.cloned.1.call-update) | async-done | bytes 4112 | tf_op jit(solution)/shard_map/reduce_scatter | solution.py:88
  859.0 1.3 add_convert_fusion
  (41 shorter events, 0.6 us)
Async XLA Ops:
  7.2 2.9 copy-start
  7.2 56.6 %all-gather.2.cloned.1.call-start = ((), (), s32[]{:S(2)}) async-start(), calls=%async_computation.1 | async-start | bytes 4325376 | tf_op jit(solution)/shard_map/all_gather | solution.py:10
  10.0 104.3 %copy-start.1 = (bf16[8,2,128,128]{3,2,1,0:T(8,128)(2,1)}, bf16[8,2,128,128]{3,2,1,0:T(8,128)(2,1)S(1)}, u32[]{:S(2)}) copy-start(bf16[8,2,128,128]{3,2,1,0:T(8,128)(2,1)S(1)} %get-tuple-element.62) | copy-start | bytes 1572868
  10.1 104.3 %copy-start.2 = (bf16[8,2,128,128]{3,2,1,0:T(8,128)(2,1)}, bf16[8,2,128,128]{3,2,1,0:T(8,128)(2,1)S(1)}, u32[]{:S(2)}) copy-start(bf16[8,2,128,128]{3,2,1,0:T(8,128)(2,1)S(1)} %get-tuple-element.61) | copy-start | bytes 1572868
  10.1 104.3 %copy-start.3 = (f32[8,128]{1,0:T(8,128)S(1)}, f32[8,128]{1,0:T(8,128)}, u32[]{:S(2)}) copy-start(f32[8,128]{1,0:T(8,128)} %param.22) | copy-start | bytes 12292
  11.8 847.2 %reduce-scatter.2.cloned.1.call-start = ((), (), s32[]{:S(2)}) async-start(), calls=%async_computation.2 | async-start | bytes 528384 | tf_op jit(solution)/shard_map/reduce_scatter | solution.py:88
  63.8 117.9 %copy-start.4 = (f32[128]{0:T(128)S(1)}, f32[128]{0:T(128)}, u32[]{:S(2)}) copy-start(f32[128]{0:T(128)} %param.23) | copy-start | bytes 1540
Sparse Core Ops, SparseCore 0:
  11.9 49.9 all-gather.1
  230.6 628.3 reduce-scatter.1
where the time goes:
time: 874 us; the launch traced here: 867 us
  waiting for transfers between devices  629 us (72%)
  blocking collectives  159 us (18%)
  other arithmetic  38.3 us (4%)
  matrix products  19.8 us (2%)
  between operations  14.2 us (2%)
    reduce_scatter x1, waiting for transfers between devices, body(): lax.psum_scatter(partial_down, ('kvh', 'seq'), scatter_dimension=1, tiled...  629 us
    psum x1, blocking collectives, body(): square = lax.psum(jnp.sum(mixed * mixed, axis=1), ('kvh', 'seq'))  64.2 us
    all_gather x2, blocking collectives, merged(): pieces = jax.tree.map(lambda part: lax.all_gather(part, axis), value)  51.5 us
    all_gather x1, blocking collectives, body(): normed = lax.all_gather(normed_share, ('kvh', 'seq'), axis=1, tiled=True)  33.6 us
    add x31, other arithmetic, combine_partials(): summed_one * weight_one[..., None] + summed_two * weight_two[..., None]  33.3 us
  transfers between devices with their start and end apart: 2, of which 1 were waited for; matrix products, arithmetic and copies ran while one was open for 0% of the time, Pallas kernels for 0%

commit v1 on v0

v1 whole, which is shorter than its diff:
```python
import functools

import jax
import jax.numpy as jnp
from jax import lax
from jax.experimental import pallas as pl
from jax.experimental.pallas import tpu as pltpu
from jax.sharding import PartitionSpec as P

F32 = jnp.float32
BF16 = jnp.bfloat16
EVERY = ("kvh", "seq")
VMEM = pl.BlockSpec(memory_space=pltpu.VMEM)
SMEM = pl.BlockSpec(memory_space=pltpu.SMEM)
ANY = pl.BlockSpec(memory_space=pl.ANY)
MIB = 1 << 20
CHUNK = 2048


def nt_dot(a, b):
    return lax.dot_general(a, b, (((1,), (1,)), ((), ())), preferred_element_type=F32)


def attention_kernel(
    new_block, fill, queries, keys, values, new_keys, new_values, keys_out, values_out, payload, rows_f32
):
    batch, heads_local, head_dim = queries.shape
    kv_local, rows = keys.shape[1], keys.shape[2]
    group = heads_local // kv_local
    block = lax.axis_index("seq")
    keys_out[...] = keys[...]
    values_out[...] = values[...]
    for b in range(batch):

        @pl.when(new_block[b] == block)
        def _():
            start = pl.multiple_of((fill[b] // 16) * 16, 16)
            hit = lax.broadcasted_iota(jnp.int32, (16, head_dim), 0) == fill[b] - start
            for k in range(kv_local):
                for new, out in ((new_keys, keys_out), (new_values, values_out)):
                    old = out[b, k, pl.ds(start, 16), :].astype(F32)
                    row = new[b, k : k + 1, :].astype(F32)
                    out[b, k, pl.ds(start, 16), :] = jnp.where(hit, row, old).astype(BF16)

    lane = lax.broadcasted_iota(jnp.int32, (group, rows), 1)
    for b in range(batch):
        target = jnp.where(new_block[b] == block, fill[b], -1)
        live = (lane < fill[b]) | (lane == target)
        for k in range(kv_local):
            query = queries[b, k * group : (k + 1) * group, :]
            scores = nt_dot(query, keys_out[b, k]) * head_dim ** (-0.5)
            scores = jnp.where(live, scores, -1e30)
            top = jnp.max(scores, axis=1, keepdims=True).astype(BF16).astype(F32)
            weights = jnp.where(live, jnp.exp(scores - top), 0.0).astype(BF16)
            total = jnp.sum(weights.astype(F32), axis=1, keepdims=True)
            summed = jnp.dot(weights, values_out[b, k], preferred_element_type=F32)
            high = total.astype(BF16).astype(F32)
            stats = jnp.where(lane < 32, top, jnp.where(lane < 64, high, total - high))
            base = k * group * 16 + b
            rows_f32[pl.ds(base, group, stride=16), :] = summed
            rows_f32[pl.ds(base + 8, group, stride=16), :] = stats
    payload[...] = rows_f32[...].reshape(heads_local, 16, head_dim).astype(BF16)


def combine_kernel(parts, out):
    sources = parts.shape[0]
    tiles = [parts[s].astype(F32) for s in range(sources)]
    stats = [t[8:16] for t in tiles]
    top = functools.reduce(jnp.maximum, stats)
    weights = [jnp.exp(jnp.minimum(s - top, 0.0)) for s in stats]
    total = 0.0
    for s, w in zip(stats, weights):
        total = total + w * (pltpu.roll(s, 96, 1) + pltpu.roll(s, 64, 1))
    scale = 1.0 / total
    heads = 0.0
    for t, w in zip(tiles, weights):
        heads = heads + t[0:8] * (w * scale)[:, 0:1]
    heads = heads.astype(BF16)
    for p in range(out.shape[0]):
        out[p] = heads


def lanes(tiles, first, count):
    return jnp.concatenate([tiles[first + i] for i in range(count)], axis=1)


def project_kernel(heads, residual, gain, weight, mixed_out, payload, buffer, sems):
    depth = weight.shape[0]
    chunks = depth // CHUNK
    per = CHUNK // 128
    copies = []
    for c in range(chunks):
        part = pl.ds(c * CHUNK, CHUNK)
        copy = pltpu.make_async_copy(weight.at[part, :], buffer.at[part, :], sems.at[c])
        copy.start()
        copies.append(copy)
    total = residual[...]
    for c in range(chunks):
        copies[c].wait()
        total = total + jnp.dot(
            lanes(heads, c * per, per), buffer[pl.ds(c * CHUNK, CHUNK), :], preferred_element_type=F32
        )
    mixed_out[...] = total
    square = jnp.sum(total * total, axis=1, keepdims=True)
    high = square.astype(BF16).astype(F32)
    lane = lax.broadcasted_iota(jnp.int32, total.shape, 1)
    stats = jnp.where(lane < 64, high, square - high)
    tile = jnp.concatenate([total * gain[...], stats], axis=0).astype(BF16)
    for p in range(payload.shape[0]):
        payload[p] = tile


def feed_kernel(tiles, gate, up, down, out, gate_buf, up_buf, down_buf, sems):
    features = gate.shape[1]
    chunks = features // CHUNK
    per = CHUNK // 128
    copies = {}
    for c in range(chunks):
        part = pl.ds(c * CHUNK, CHUNK)
        for kind, (source, target) in enumerate(((gate, gate_buf), (up, up_buf))):
            copies[kind, c] = pltpu.make_async_copy(source.at[:, part], target.at[c], sems.at[kind, c])
            copies[kind, c].start()
    for c in range(chunks):
        copies[2, c] = pltpu.make_async_copy(down.at[:, pl.ds(c * CHUNK, CHUNK)], down_buf.at[c], sems.at[2, c])
        copies[2, c].start()
    squares = 0.0
    for p in range(tiles.shape[0]):
        squares = squares + tiles[p].astype(F32)
    squares = squares[8:16]
    squares = squares + pltpu.roll(squares, 64, 1)
    factor = lax.rsqrt(squares[:, 0:1] / features + 1e-05)
    gate_sum = 0.0
    up_sum = 0.0
    for c in range(chunks):
        piece = lanes(tiles, c * per, per)
        copies[0, c].wait()
        gate_sum = gate_sum + nt_dot(piece, gate_buf[c])
        copies[1, c].wait()
        up_sum = up_sum + nt_dot(piece, up_buf[c])
    gate_sum = gate_sum[0:8] * factor
    up_sum = up_sum[0:8] * factor
    hidden = (gate_sum / (1.0 + jnp.exp(-gate_sum)) * up_sum).astype(BF16)
    for c in range(chunks):
        copies[2, c].wait()
        sums = jnp.dot(hidden, down_buf[c], preferred_element_type=F32).astype(BF16)
        for i in range(per):
            out[c * per + i] = sums[:, i * 128 : (i + 1) * 128]


def finish_kernel(sums, mixed, out):
    total = mixed[...]
    for p in range(sums.shape[0]):
        total = total + sums[p].astype(F32)
    out[...] = total.astype(BF16)


def body(
    queries,
    key_cache,
    value_cache,
    new_keys,
    new_values,
    block_fill,
    new_block,
    residual,
    norm_gain,
    out_weight,
    gate_weight,
    up_weight,
    down_weight,
):
    batch, heads_local, head_dim = queries.shape
    devices = lax.axis_size("kvh") * lax.axis_size("seq")
    hidden, features = gate_weight.shape
    chunks = features // CHUNK
    columns = residual.shape[1]

    keys_out, values_out, partials = pl.pallas_call(
        attention_kernel,
        out_shape=(
            jax.ShapeDtypeStruct(key_cache.shape, BF16),
            jax.ShapeDtypeStruct(value_cache.shape, BF16),
            jax.ShapeDtypeStruct((heads_local, 16, head_dim), BF16),
        ),
        in_specs=[SMEM, SMEM] + [VMEM] * 5,
        out_specs=(VMEM, VMEM, VMEM),
        scratch_shapes=[pltpu.VMEM((heads_local * 16, head_dim), F32)],
        compiler_params=pltpu.CompilerParams(vmem_limit_bytes=8 * MIB),
        name="attention",
    )(new_block, block_fill.reshape(batch), queries, key_cache, value_cache, new_keys, new_values)
    partials = lax.all_to_all(partials, "seq", 0, 0)

    heads = pl.pallas_call(
        combine_kernel,
        out_shape=jax.ShapeDtypeStruct((devices, batch, head_dim), BF16),
        in_specs=[VMEM],
        out_specs=VMEM,
        compiler_params=pltpu.CompilerParams(vmem_limit_bytes=4 * MIB),
        name="combine",
    )(partials)
    heads = lax.all_to_all(heads, EVERY, 0, 0)

    mixed, stream = pl.pallas_call(
        project_kernel,
        out_shape=(
            jax.ShapeDtypeStruct((batch, columns), F32),
            jax.ShapeDtypeStruct((devices, 2 * batch, columns), BF16),
        ),
        in_specs=[VMEM, VMEM, VMEM, ANY],
        out_specs=(VMEM, VMEM),
        scratch_shapes=[
            pltpu.VMEM(out_weight.shape, BF16),
            pltpu.SemaphoreType.DMA((out_weight.shape[0] // CHUNK,)),
        ],
        compiler_params=pltpu.CompilerParams(vmem_limit_bytes=12 * MIB),
        name="project",
    )(heads, residual, norm_gain.reshape(1, columns), out_weight)
    stream = lax.all_to_all(stream, EVERY, 0, 0)

    sums = pl.pallas_call(
        feed_kernel,
        out_shape=jax.ShapeDtypeStruct((devices, batch, columns), BF16),
        in_specs=[VMEM, ANY, ANY, ANY],
        out_specs=VMEM,
        scratch_shapes=[pltpu.VMEM((chunks, hidden, CHUNK), BF16)] * 3 + [pltpu.SemaphoreType.DMA((3, chunks))],
        compiler_params=pltpu.CompilerParams(vmem_limit_bytes=32 * MIB),
        name="feed",
    )(stream, gate_weight, up_weight, down_weight)
    sums = lax.all_to_all(sums, EVERY, 0, 0)

    layer_out = pl.pallas_call(
        finish_kernel,
        out_shape=jax.ShapeDtypeStruct((batch, columns), BF16),
        in_specs=[VMEM, VMEM],
        out_specs=VMEM,
        compiler_params=pltpu.CompilerParams(vmem_limit_bytes=4 * MIB),
        name="finish",
    )(sums, mixed)
    return (layer_out, keys_out, values_out)


def solution(mesh):
    placed = (
        P(None, "kvh", None),
        P(None, "kvh", "seq", None),
        P(None, "kvh", "seq", None),
        P(None, "kvh", None),
        P(None, "kvh", None),
        P(None, "seq"),
        P(),
        P(None, ("kvh", "seq")),
        P(("kvh", "seq")),
        P(None, ("kvh", "seq")),
        P(("kvh", "seq"), None),
        P(("kvh", "seq"), None),
        P(("kvh", "seq"), None),
    )
    return jax.shard_map(
        body,
        mesh=mesh,
        in_specs=placed,
        out_specs=(
            P(None, ("kvh", "seq")),
            P(None, "kvh", "seq", None),
            P(None, "kvh", "seq", None),
        ),
        check_vma=False,
    )
```

time: 874 us -> 103 us (0.12)
  waiting for transfers between devices: 629 us -> 0 us
  blocking collectives: 159 us -> 66.9 us
  other arithmetic: 38.3 us -> 0 us
  matrix products: 19.8 us -> 0 us
  Pallas kernels: 0 us -> 19.4 us
  between operations: 14.2 us -> 0.69 us
  local copies, waits for them, and re-layouts: 5.88 us -> 15.4 us
    reduce_scatter x1 -> x0, waiting for transfers between devices: 629 us -> none  [body(): lax.psum_scatter(partial_down, ('kvh', 'seq'), scatter_dimension=1, tiled...]
    all_gather x4 -> x0, blocking collectives: 95.3 us -> none  [the longest x2 51.5 us: merged(): pieces = jax.tree.map(lambda part: lax.all_gather(part, axis), value)]
    all_to_all x0 -> x4, blocking collectives: none -> 66.9 us  [the longest x1 18.1 us: body(): stream = lax.all_to_all(stream, EVERY, 0, 0)]
    psum x1 -> x0, blocking collectives: 64.2 us -> none  [body(): square = lax.psum(jnp.sum(mixed * mixed, axis=1), ('kvh', 'seq'))]
    add x62 -> x0, other arithmetic: 33.8 us -> none  [the longest x31 33.3 us: combine_partials(): summed_one * weight_one[..., None] + summed_two * weight_two[..., None]]
    dot_general x5 -> x0, matrix products: 19.8 us -> none  [the longest x1 10.3 us: body(): jnp.dot(hidden, down_weight, preferred_element_type=jnp.float32)]
    pallas_call x0 -> x5, Pallas kernels: none -> 19.4 us  [the longest x1 11.9 us: body(): pl.pallas_call(feed_kernel, out_shape=jax.ShapeDtypeStruct((devices, batc...]
    unnamed x10 -> x26, local copies, waits for them, and re-layouts: 0.04 us -> 15.4 us
  transfers between devices with their start and end apart: 2 -> 0, of which waited for: 1 -> 0; matrix products, arithmetic and copies ran while one was open for 0% -> 0% of each run, Pallas kernels for 0% -> 0%
where the time goes in v1:
time: 103 us; the launch traced here: 102 us
  blocking collectives  66.9 us (65%)
  Pallas kernels  19.4 us (19%)
  local copies, waits for them, and re-layouts  15.4 us (15%)
    all_to_all x1, blocking collectives, body(): stream = lax.all_to_all(stream, EVERY, 0, 0)  18.1 us
    all_to_all x1, blocking collectives, body(): partials = lax.all_to_all(partials, 'seq', 0, 0)  17.1 us
    all_to_all x1, blocking collectives, body(): heads = lax.all_to_all(heads, EVERY, 0, 0)  16.4 us
    unnamed x26, local copies, waits for them, and re-layouts  15.4 us
    all_to_all x1, blocking collectives, body(): sums = lax.all_to_all(sums, EVERY, 0, 0)  15.3 us
    pallas_call x1, Pallas kernels, body(): pl.pallas_call(feed_kernel, out_shape=jax.ShapeDtypeStruct((devices, batc...  11.9 us
    pallas_call x1, Pallas kernels, body(): pl.pallas_call(attention_kernel, out_shape=(jax.ShapeDtypeStruct(key_cach...  4.57 us

profile of v1, /device:TPU:1, one launch (start us, length us, event | category | flops | bytes accessed | tf_op | source)
XLA Modules:
  0.0 102.3 jit_solution(9231471362824805903)
XLA Ops:
  0.6 0.0 copy-start
  0.6 0.0 copy-start.4
  0.7 1.2 %copy-done.4 = bf16[8,2,128,128]{3,2,1,0:T(8,128)(2,1)S(1)} copy-done((bf16[8,2,128,128]{3,2,1,0:T(8,128)(2,1)S(1)}, bf16[8,2,128,128]{3,2,1,0:T(8,128)(2,1)}, u32[]{:S(2)}) %copy-start.4) | copy-done | bytes 524312
  1.8 0.0 copy-start.5
  1.8 1.3 %copy-done.5 = bf16[8,2,128,128]{3,2,1,0:T(8,128)(2,1)S(1)} copy-done((bf16[8,2,128,128]{3,2,1,0:T(8,128)(2,1)S(1)}, bf16[8,2,128,128]{3,2,1,0:T(8,128)(2,1)}, u32[]{:S(2)}) %copy-start.5) | copy-done | bytes 524312
  3.1 0.0 copy-start.6
  3.1 0.8 copy-done.6
  3.9 0.0 copy-start.7
  3.9 0.7 copy-done.7
  4.6 0.0 copy-start.8
  4.6 0.7 copy-done.8
  5.3 0.0 copy-start.10
  5.3 0.7 copy-done.10
  6.0 0.0 copy-start.11
  6.0 0.7 copy-done.11
  6.6 4.6 %attention.1 = (bf16[8,2,128,128]{3,2,1,0:T(8,128)(2,1)}, bf16[8,2,128,128]{3,2,1,0:T(8,128)(2,1)}, bf16[32,16,128]{2,1,0:T(8,128)(2,1)S(1)}) custom-call(s32[8]{0:T(128)S(1)} %copy-done.10, s32[8]{0:T(128)S(1)} %bitcast.2, bf16[8,32,128]{2,1,0:T(8,128)(2,1)S(1)} %copy-done.6, bf16[8,2,128,128]{3,2,1,0:T(8,128)(2,1)S(1)} %copy-done.4, ...), custom_call_target="tpu_custom_call" | custom-call | tf_op jit(solution)/shard_map/attention/pallas_call | solution.py:178
  11.2 17.1 %all_to_all.20.parts = bf16[32,16,128]{2,1,0:T(8,128)(2,1)S(1)} all-to-all(bf16[32,16,128]{2,1,0:T(8,128)(2,1)S(1)} %get-tuple-element.8), channel_id=1, replica_groups=mesh['kvh'=4,'seq'=32] {'seq'}, dimensions={0} | all-to-all | bytes 262144 | tf_op jit(solution)/shard_map/all_to_all | solution.py:191
  28.3 0.2 combine.1
  28.6 16.4 %all_to_all.21.heads = bf16[128,8,128]{2,1,0:T(8,128)(2,1)S(1)} all-to-all(bf16[128,8,128]{2,1,0:T(8,128)(2,1)S(1)} %combine.1), channel_id=1, replica_groups=mesh['kvh'=4,'seq'=32] {'kvh','seq'}, dimensions={0} | all-to-all | bytes 524288 | tf_op jit(solution)/shard_map/all_to_all | solution.py:201
  45.0 0.0 copy-start.3
  45.0 2.2 %copy-done.3 = bf16[16384,128]{1,0:T(8,128)(2,1)S(1)} copy-done((bf16[16384,128]{1,0:T(8,128)(2,1)S(1)}, bf16[16384,128]{1,0:T(8,128)(2,1)}, u32[]{:S(2)}) %copy-start.3) | copy-done | bytes 4194328
  47.1 0.0 copy-start.9
  47.1 0.7 copy-done.9
  47.8 0.0 copy-start.12
  47.8 0.7 copy-done.12
  48.5 2.0 %project.1 = (f32[8,128]{1,0:T(8,128)S(1)}, bf16[128,16,128]{2,1,0:T(8,128)(2,1)S(1)}) custom-call(bf16[128,8,128]{2,1,0:T(8,128)(2,1)S(1)} %all_to_all.21.heads, f32[8,128]{1,0:T(8,128)S(1)} %copy-done.9, f32[1,128]{1,0:T(1,128)S(1)} %bitcast.3, bf16[16384,128]{1,0:T(8,128)(2,1)S(1)} %copy-done.3), custom_call_target="tpu_custom_call" | custom-call | tf_op jit(solution)/shard_map/project/pallas_call | solution.py:203
  50.5 18.1 %all_to_all.22.tiles = bf16[128,16,128]{2,1,0:T(8,128)(2,1)S(1)} all-to-all(bf16[128,16,128]{2,1,0:T(8,128)(2,1)S(1)} %get-tuple-element.9), channel_id=1, replica_groups=mesh['kvh'=4,'seq'=32] {'kvh','seq'}, dimensions={0} | all-to-all | bytes 1048576 | tf_op jit(solution)/shard_map/all_to_all | solution.py:218
  68.6 0.0 copy-done
  68.6 0.0 copy-start.1
  68.6 2.9 %copy-done.1 = bf16[208,16384]{1,0:T(8,128)(2,1)S(1)} copy-done((bf16[208,16384]{1,0:T(8,128)(2,1)S(1)}, bf16[208,16384]{1,0:T(8,128)(2,1)}, u32[]{:S(2)}) %copy-start.1) | copy-done | bytes 6815768
  71.5 0.0 copy-start.2
  71.5 2.9 %copy-done.2 = bf16[208,16384]{1,0:T(8,128)(2,1)S(1)} copy-done((bf16[208,16384]{1,0:T(8,128)(2,1)S(1)}, bf16[208,16384]{1,0:T(8,128)(2,1)}, u32[]{:S(2)}) %copy-start.2) | copy-done | bytes 6815768
  74.4 11.9 %feed.1 = bf16[128,8,128]{2,1,0:T(8,128)(2,1)S(1)} custom-call(bf16[128,16,128]{2,1,0:T(8,128)(2,1)S(1)} %all_to_all.22.tiles, bf16[208,16384]{1,0:T(8,128)(2,1)S(1)} %copy-done, bf16[208,16384]{1,0:T(8,128)(2,1)S(1)} %copy-done.1, bf16[208,16384]{1,0:T(8,128)(2,1)S(1)} %copy-done.2), custom_call_target="tpu_custom_call" | custom-call | tf_op jit(solution)/shard_map/feed/pallas_call | solution.py:220
  86.3 15.3 %all_to_all.23.sums = bf16[128,8,128]{2,1,0:T(8,128)(2,1)S(1)} all-to-all(bf16[128,8,128]{2,1,0:T(8,128)(2,1)S(1)} %feed.1), channel_id=1, replica_groups=mesh['kvh'=4,'seq'=32] {'kvh','seq'}, dimensions={0} | all-to-all | bytes 524288 | tf_op jit(solution)/shard_map/all_to_all | solution.py:229
  101.6 0.7 finish.1
Async XLA Ops:
  0.6 67.9 %copy-start = (bf16[208,16384]{1,0:T(8,128)(2,1)S(1)}, bf16[208,16384]{1,0:T(8,128)(2,1)}, u32[]{:S(2)}) copy-start(bf16[208,16384]{1,0:T(8,128)(2,1)} %gate.1) | copy-start | bytes 20447236
  0.6 1.2 %copy-start.4 = (bf16[8,2,128,128]{3,2,1,0:T(8,128)(2,1)S(1)}, bf16[8,2,128,128]{3,2,1,0:T(8,128)(2,1)}, u32[]{:S(2)}) copy-start(bf16[8,2,128,128]{3,2,1,0:T(8,128)(2,1)} %keys.1) | copy-start | bytes 1572868
  1.8 1.3 %copy-start.5 = (bf16[8,2,128,128]{3,2,1,0:T(8,128)(2,1)S(1)}, bf16[8,2,128,128]{3,2,1,0:T(8,128)(2,1)}, u32[]{:S(2)}) copy-start(bf16[8,2,128,128]{3,2,1,0:T(8,128)(2,1)} %values.1) | copy-start | bytes 1572868
  3.1 0.8 copy-start.6
  3.9 0.7 copy-start.7
  4.6 0.7 copy-start.8
  5.3 0.7 copy-start.10
  6.0 0.7 copy-start.11
  45.0 2.2 %copy-start.3 = (bf16[16384,128]{1,0:T(8,128)(2,1)S(1)}, bf16[16384,128]{1,0:T(8,128)(2,1)}, u32[]{:S(2)}) copy-start(bf16[16384,128]{1,0:T(8,128)(2,1)} %weight.1) | copy-start | bytes 12582916
  47.1 0.7 copy-start.9
  47.8 0.7 copy-start.12
  68.6 2.9 %copy-start.1 = (bf16[208,16384]{1,0:T(8,128)(2,1)S(1)}, bf16[208,16384]{1,0:T(8,128)(2,1)}, u32[]{:S(2)}) copy-start(bf16[208,16384]{1,0:T(8,128)(2,1)} %up.1) | copy-start | bytes 20447236
  71.5 2.9 %copy-start.2 = (bf16[208,16384]{1,0:T(8,128)(2,1)S(1)}, bf16[208,16384]{1,0:T(8,128)(2,1)}, u32[]{:S(2)}) copy-start(bf16[208,16384]{1,0:T(8,128)(2,1)} %down.1) | copy-start | bytes 20447236

commit v2 on v0

v2 whole, which is shorter than its diff:
```python
import functools

import jax
import jax.numpy as jnp
from jax import lax
from jax.experimental import pallas as pl
from jax.experimental.pallas import tpu as pltpu
from jax.sharding import PartitionSpec as P

F32 = jnp.float32
BF16 = jnp.bfloat16
EVERY = ("kvh", "seq")
VMEM = pl.BlockSpec(memory_space=pltpu.VMEM)
ANY = pl.BlockSpec(memory_space=pl.ANY)
MIB = 1 << 20
CHUNK = 2048
COST = pl.CostEstimate(flops=20 * 10**9, bytes_accessed=60 * 10**6, transcendentals=20 * 10**6)


def nt_dot(a, b):
    return lax.dot_general(a, b, (((1,), (1,)), ((), ())), preferred_element_type=F32)


def tree_sum(terms):
    terms = list(terms)
    while len(terms) > 1:
        paired = [a + b for a, b in zip(terms[0::2], terms[1::2])]
        terms = paired + terms[len(paired) * 2 :]
    return terms[0]


def start_copies(pairs, sems, first=0):
    copies = [pltpu.make_async_copy(src, dst, sems.at[first + i]) for i, (src, dst) in enumerate(pairs)]
    for copy in copies:
        copy.start()
    return copies


def wait_copies(copies):
    for copy in copies:
        copy.wait()


def place_rows(block, new_block, fill, caches):
    batch, kv_local, _, head_dim = caches[0][1].shape
    for b in range(batch):

        @pl.when(new_block[b] == block)
        def _():
            start = pl.multiple_of((fill[b] // 16) * 16, 16)
            hit = lax.broadcasted_iota(jnp.int32, (16, head_dim), 0) == fill[b] - start
            for k in range(kv_local):
                for new, cache in caches:
                    old = cache[b, k, pl.ds(start, 16), :].astype(F32)
                    row = new[b, k : k + 1, :].astype(F32)
                    cache[b, k, pl.ds(start, 16), :] = jnp.where(hit, row, old).astype(BF16)


def attention_kernel(
    new_block_hbm,
    fill_hbm,
    queries_hbm,
    keys_hbm,
    values_hbm,
    new_keys_hbm,
    new_values_hbm,
    payload,
    keys_out,
    values_out,
    new_block,
    fill,
    queries,
    keys,
    values,
    new_keys,
    new_values,
    rows_f32,
    sems,
):
    batch, heads_local, head_dim = queries.shape
    kv_local, rows = keys.shape[1], keys.shape[2]
    group = heads_local // kv_local
    block = lax.axis_index("seq")
    copies = start_copies(
        (
            (keys_hbm, keys),
            (values_hbm, values),
            (queries_hbm, queries),
            (new_keys_hbm, new_keys),
            (new_values_hbm, new_values),
            (new_block_hbm, new_block),
            (fill_hbm, fill),
        ),
        sems,
    )
    wait_copies(copies)
    place_rows(block, new_block, fill, ((new_keys, keys), (new_values, values)))
    writes = start_copies(((keys, keys_out), (values, values_out)), sems, len(copies))

    lane = lax.broadcasted_iota(jnp.int32, (group, rows), 1)
    places = [(b, k) for b in range(batch) for k in range(kv_local)]
    live = [lane < fill[b] + jnp.where(new_block[b] == block, 1, 0) for b in range(batch)]
    scores = [nt_dot(queries[b, k * group : (k + 1) * group, :], keys[b, k]) for b, k in places]
    scores = [jnp.where(live[b], s * head_dim ** (-0.5), -1e30) for (b, _), s in zip(places, scores)]
    tops = [jnp.max(s, axis=1, keepdims=True).astype(BF16).astype(F32) for s in scores]
    weights = [
        jnp.where(live[b], jnp.exp(s - t), 0.0).astype(BF16) for (b, _), s, t in zip(places, scores, tops)
    ]
    sums = [jnp.dot(w, values[b, k], preferred_element_type=F32) for (b, k), w in zip(places, weights)]
    totals = [jnp.sum(w.astype(F32), axis=1, keepdims=True) for w in weights]
    for (b, k), top, total, summed in zip(places, tops, totals, sums):
        high = total.astype(BF16).astype(F32)
        stats = jnp.where(lane < 32, top, jnp.where(lane < 64, high, total - high))
        base = k * group * 16 + b
        rows_f32[pl.ds(base, group, stride=16), :] = summed
        rows_f32[pl.ds(base + 8, group, stride=16), :] = stats
    payload[...] = rows_f32[...].reshape(heads_local, 16, head_dim).astype(BF16)
    wait_copies(writes)


def combine_kernel(parts, out):
    sources = parts.shape[0]
    tiles = [parts[s].astype(F32) for s in range(sources)]
    stats = [t[8:16] for t in tiles]
    top = functools.reduce(jnp.maximum, stats)
    weights = [jnp.exp(jnp.minimum(s - top, 0.0)) for s in stats]
    total = tree_sum(w * (pltpu.roll(s, 96, 1) + pltpu.roll(s, 64, 1)) for s, w in zip(stats, weights))
    scale = 1.0 / total
    heads = tree_sum(t[0:8] * (w * scale)[:, 0:1] for t, w in zip(tiles, weights)).astype(BF16)
    for p in range(out.shape[0]):
        out[p] = heads


def project_kernel(heads, residual, gain, weight, mixed_out, payload):
    per = CHUNK // 128
    total = residual[...] + tree_sum(
        jnp.dot(
            jnp.concatenate([heads[c * per + i] for i in range(per)], axis=1),
            weight[c * CHUNK : (c + 1) * CHUNK, :],
            preferred_element_type=F32,
        )
        for c in range(weight.shape[0] // CHUNK)
    )
    mixed_out[...] = total
    square = jnp.sum(total * total, axis=1, keepdims=True)
    high = square.astype(BF16).astype(F32)
    low = square - high
    lane = lax.broadcasted_iota(jnp.int32, (2, total.shape[1]), 1)
    stats = jnp.zeros(lane.shape, F32)
    for b in range(total.shape[0]):
        stats = jnp.where(lane == b, high[b : b + 1], jnp.where(lane == 64 + b, low[b : b + 1], stats))
    tile = jnp.concatenate([total * gain[...], stats], axis=0).astype(BF16)
    for j in range(payload.shape[1]):
        pair = tile[2 * j : 2 * j + 2]
        for p in range(payload.shape[0]):
            payload[p, j] = pair


def feed_kernel(tiles, gate, up, down, out):
    features = gate.shape[1]
    chunks = features // CHUNK
    per = CHUNK // 128
    squares = tree_sum(tiles[p, 4].astype(F32) for p in range(tiles.shape[0]))
    squares = squares + pltpu.roll(squares, 64, 1)
    factor = jnp.concatenate([lax.rsqrt(squares[0:1, b : b + 1] / features + 1e-05) for b in range(8)], axis=0)
    gate_sum = 0.0
    up_sum = 0.0
    for c in range(chunks):
        piece = jnp.concatenate(
            [jnp.concatenate([tiles[c * per + i, j] for j in range(4)], axis=0) for i in range(per)], axis=1
        )
        part = slice(c * CHUNK, (c + 1) * CHUNK)
        gate_sum = gate_sum + nt_dot(gate[:, part], piece)
        up_sum = up_sum + nt_dot(up[:, part], piece)
    gate_sum = gate_sum.T * factor
    up_sum = up_sum.T * factor
    hidden = (gate_sum / (1.0 + jnp.exp(-gate_sum)) * up_sum).astype(BF16)
    for c in range(chunks):
        sums = jnp.dot(hidden, down[:, c * CHUNK : (c + 1) * CHUNK], preferred_element_type=F32).astype(BF16)
        for i in range(per):
            out[c * per + i] = sums[:, i * 128 : (i + 1) * 128]


def finish_kernel(sums, mixed, out):
    total = tree_sum(sums[p].astype(F32) for p in range(sums.shape[0]))
    out[...] = (mixed[...] + total).astype(BF16)


def in_hbm(x):
    return pltpu.with_memory_space_constraint(x, pltpu.HBM)


def call(kernel, name, operands, in_specs, out_shape, out_specs, scratch=()):
    return pl.pallas_call(
        kernel,
        out_shape=out_shape,
        in_specs=in_specs,
        out_specs=out_specs,
        scratch_shapes=list(scratch),
        compiler_params=pltpu.CompilerParams(vmem_limit_bytes=4 * MIB),
        cost_estimate=COST,
        name=name,
    )(*operands)


def body(
    queries,
    key_cache,
    value_cache,
    new_keys,
    new_values,
    block_fill,
    new_block,
    residual,
    norm_gain,
    out_weight,
    gate_weight,
    up_weight,
    down_weight,
):
    batch, heads_local, head_dim = queries.shape
    devices = lax.axis_size("kvh") * lax.axis_size("seq")
    columns = residual.shape[1]
    fill = block_fill.reshape(batch)
    counts = [pltpu.SMEM((batch,), jnp.int32)] * 2
    caches = [pltpu.VMEM(key_cache.shape, BF16)] * 2
    fresh = [pltpu.VMEM(new_keys.shape, BF16)] * 2

    partials, keys_out, values_out = call(
        attention_kernel,
        "attention",
        [*map(in_hbm, (new_block, fill, queries, key_cache, value_cache, new_keys, new_values))],
        [ANY] * 7,
        (
            jax.ShapeDtypeStruct((heads_local, 16, head_dim), BF16),
            jax.ShapeDtypeStruct(key_cache.shape, BF16),
            jax.ShapeDtypeStruct(value_cache.shape, BF16),
        ),
        (VMEM, ANY, ANY),
        [
            *counts,
            pltpu.VMEM(queries.shape, BF16),
            *caches,
            *fresh,
            pltpu.VMEM((heads_local * 16, head_dim), F32),
            pltpu.SemaphoreType.DMA((9,)),
        ],
    )
    gathered = lax.all_to_all(partials, "seq", 0, 0)
    heads = call(
        combine_kernel,
        "combine",
        [gathered],
        [VMEM],
        jax.ShapeDtypeStruct((devices, batch, head_dim), BF16),
        VMEM,
    )
    all_heads = lax.all_to_all(heads, EVERY, 0, 0)
    mixed, stream = call(
        project_kernel,
        "project",
        [all_heads, residual, norm_gain.reshape(1, columns), out_weight],
        [VMEM] * 4,
        (
            jax.ShapeDtypeStruct((batch, columns), F32),
            jax.ShapeDtypeStruct((devices, batch // 2 + 1, 2, columns), BF16),
        ),
        (VMEM, VMEM),
    )
    all_stream = lax.all_to_all(stream, EVERY, 0, 0)
    sums = call(
        feed_kernel,
        "feed",
        [all_stream, gate_weight, up_weight, down_weight],
        [VMEM] * 4,
        jax.ShapeDtypeStruct((devices, batch, columns), BF16),
        VMEM,
    )
    all_sums = lax.all_to_all(sums, EVERY, 0, 0)
    layer_out = call(
        finish_kernel,
        "finish",
        [all_sums, mixed],
        [VMEM] * 2,
        jax.ShapeDtypeStruct((batch, columns), BF16),
        VMEM,
    )
    return (layer_out, keys_out, values_out)


def solution(mesh):
    placed = (
        P(None, "kvh", None),
        P(None, "kvh", "seq", None),
        P(None, "kvh", "seq", None),
        P(None, "kvh", None),
        P(None, "kvh", None),
        P(None, "seq"),
        P(),
        P(None, ("kvh", "seq")),
        P(("kvh", "seq")),
        P(None, ("kvh", "seq")),
        P(("kvh", "seq"), None),
        P(("kvh", "seq"), None),
        P(("kvh", "seq"), None),
    )
    return jax.shard_map(
        body,
        mesh=mesh,
        in_specs=placed,
        out_specs=(
            P(None, ("kvh", "seq")),
            P(None, "kvh", "seq", None),
            P(None, "kvh", "seq", None),
        ),
        check_vma=False,
    )
```

time: 874 us -> 74.7 us (0.09)
  waiting for transfers between devices: 629 us -> 0 us
  blocking collectives: 159 us -> 64.9 us
  other arithmetic: 38.3 us -> 0.01 us
  matrix products: 19.8 us -> 0 us
  between operations: 14.2 us -> 0.76 us
  Pallas kernels: 0 us -> 8.84 us
    reduce_scatter x1 -> x0, waiting for transfers between devices: 629 us -> none  [body(): lax.psum_scatter(partial_down, ('kvh', 'seq'), scatter_dimension=1, tiled...]
    all_gather x4 -> x0, blocking collectives: 95.3 us -> none  [the longest x2 51.5 us: merged(): pieces = jax.tree.map(lambda part: lax.all_gather(part, axis), value)]
    all_to_all x0 -> x4, blocking collectives: none -> 64.9 us  [the longest x1 17.1 us: body(): gathered = lax.all_to_all(partials, 'seq', 0, 0)]
    psum x1 -> x0, blocking collectives: 64.2 us -> none  [body(): square = lax.psum(jnp.sum(mixed * mixed, axis=1), ('kvh', 'seq'))]
    add x62 -> x0, other arithmetic: 33.8 us -> none  [the longest x31 33.3 us: combine_partials(): summed_one * weight_one[..., None] + summed_two * weight_two[..., None]]
    dot_general x5 -> x0, matrix products: 19.8 us -> none  [the longest x1 10.3 us: body(): jnp.dot(hidden, down_weight, preferred_element_type=jnp.float32)]
    pallas_call x0 -> x5, Pallas kernels: none -> 8.84 us  [call(): pl.pallas_call(kernel, out_shape=out_shape, in_specs=in_specs, out_specs=...]
  transfers between devices with their start and end apart: 2 -> 0, of which waited for: 1 -> 0; matrix products, arithmetic and copies ran while one was open for 0% -> 0% of each run, Pallas kernels for 0% -> 0%
where the time goes in v2:
time: 74.7 us; the launch traced here: 74.5 us
  blocking collectives  64.9 us (87%)
  Pallas kernels  8.84 us (12%)
  between operations  0.76 us (1%)
    all_to_all x1, blocking collectives, body(): gathered = lax.all_to_all(partials, 'seq', 0, 0)  17.1 us
    all_to_all x1, blocking collectives, body(): all_heads = lax.all_to_all(heads, EVERY, 0, 0)  16.4 us
    all_to_all x1, blocking collectives, body(): all_stream = lax.all_to_all(stream, EVERY, 0, 0)  16 us
    all_to_all x1, blocking collectives, body(): all_sums = lax.all_to_all(sums, EVERY, 0, 0)  15.4 us
    pallas_call x5, Pallas kernels, call(): pl.pallas_call(kernel, out_shape=out_shape, in_specs=in_specs, out_specs=...  8.84 us

profile of v2, /device:TPU:1, one launch (start us, length us, event | category | flops | bytes accessed | tf_op | source)
XLA Modules:
  0.0 74.5 jit_solution(9509380280848420372)
XLA Ops:
  0.6 2.3 %attention.1 = (bf16[32,16,128]{2,1,0:T(8,128)(2,1)S(1)}, bf16[8,2,128,128]{3,2,1,0:T(8,128)(2,1)}, bf16[8,2,128,128]{3,2,1,0:T(8,128)(2,1)}) custom-call(s32[8]{0:T(128)} %new_block_hbm.1, s32[8]{0:T(128)} %bitcast.9, bf16[8,32,128]{2,1,0:T(8,128)(2,1)} %queries_hbm.1, bf16[8,2,128,128]{3,2,1,0:T(8,128)(2,1)} %keys_hbm.1, ...), custom_call_target="tpu_custom_call" | custom-call | flops 20000000000 | bytes 60000000 | tf_op jit(solution)/shard_map/attention/pallas_call | solution.py:194
  3.0 17.1 %all_to_all.20.parts = bf16[32,16,128]{2,1,0:T(8,128)(2,1)S(1)} all-to-all(bf16[32,16,128]{2,1,0:T(8,128)(2,1)S(1)} %get-tuple-element.8), channel_id=1, replica_groups=mesh['kvh'=4,'seq'=32] {'seq'}, dimensions={0} | all-to-all | bytes 262144 | tf_op jit(solution)/shard_map/all_to_all | solution.py:249
  20.1 0.0 copy-start
  20.1 0.0 copy-start.1
  20.1 0.0 copy-start.2
  20.1 0.0 slice-start
  20.1 0.0 slice-start.2
  20.1 0.0 slice-start.4
  20.1 0.2 combine.1
  20.4 16.4 %all_to_all.21.heads = bf16[128,8,128]{2,1,0:T(8,128)(2,1)S(1)} all-to-all(bf16[128,8,128]{2,1,0:T(8,128)(2,1)S(1)} %combine.1), channel_id=1, replica_groups=mesh['kvh'=4,'seq'=32] {'kvh','seq'}, dimensions={0} | all-to-all | bytes 524288 | tf_op jit(solution)/shard_map/all_to_all | solution.py:258
  36.8 0.0 copy-done
  36.8 0.0 copy-done.1
  36.8 0.0 copy-done.2
  36.8 0.0 slice-start.1
  36.8 0.0 slice-start.3
  36.8 0.0 slice-start.5
  36.8 0.9 %project.1 = (f32[8,128]{1,0:T(8,128)S(1)}, bf16[128,5,2,128]{3,2,1,0:T(2,128)(2,1)S(1)}) custom-call(bf16[128,8,128]{2,1,0:T(8,128)(2,1)S(1)} %all_to_all.21.heads, f32[8,128]{1,0:T(8,128)S(1)} %copy-done.1, f32[1,128]{1,0:T(1,128)S(1)} %bitcast.8, bf16[16384,128]{1,0:T(8,128)(2,1)S(1)} %copy-done), custom_call_target="tpu_custom_call" | custom-call | flops 20000000000 | bytes 60000000 | tf_op jit(solution)/shard_map/project/pallas_call | solution.py:194
  37.8 16.0 %all_to_all.22.tiles = bf16[128,5,2,128]{3,2,1,0:T(2,128)(2,1)S(1)} all-to-all(bf16[128,5,2,128]{3,2,1,0:T(2,128)(2,1)S(1)} %get-tuple-element.9), channel_id=1, replica_groups=mesh['kvh'=4,'seq'=32] {'kvh','seq'}, dimensions={0} | all-to-all | bytes 655360 | tf_op jit(solution)/shard_map/all_to_all | solution.py:270
  53.8 0.0 slice-done
  53.8 0.0 slice-done.2
  53.8 0.0 slice-done.4
  53.8 0.0 slice-done.1
  53.8 0.0 slice-done.3
  53.8 0.0 slice-done.5
  53.8 4.7 %feed.1 = bf16[128,8,128]{2,1,0:T(8,128)(2,1)S(1)} custom-call(bf16[128,5,2,128]{3,2,1,0:T(2,128)(2,1)S(1)} %all_to_all.22.tiles, bf16[208,16384]{1,0:T(8,128)(2,1)S(1)} %bitcast.3, bf16[208,16384]{1,0:T(8,128)(2,1)S(1)} %bitcast.5, bf16[208,16384]{1,0:T(8,128)(2,1)S(1)} %bitcast.7), custom_call_target="tpu_custom_call" | custom-call | flops 20000000000 | bytes 60000000 | tf_op jit(solution)/shard_map/feed/pallas_call | solution.py:194
  58.5 15.4 %all_to_all.23.sums = bf16[128,8,128]{2,1,0:T(8,128)(2,1)S(1)} all-to-all(bf16[128,8,128]{2,1,0:T(8,128)(2,1)S(1)} %feed.1), channel_id=1, replica_groups=mesh['kvh'=4,'seq'=32] {'kvh','seq'}, dimensions={0} | all-to-all | bytes 524288 | tf_op jit(solution)/shard_map/all_to_all | solution.py:279
  73.9 0.6 finish.1
  (3 shorter events, 0.0 us)
Async XLA Ops:
  20.1 16.7 %copy-start = (bf16[16384,128]{1,0:T(8,128)(2,1)S(1)}, bf16[16384,128]{1,0:T(8,128)(2,1)}, u32[]{:S(2)}) copy-start(bf16[16384,128]{1,0:T(8,128)(2,1)} %weight.1) | copy-start | bytes 12582916
  20.1 16.7 %copy-start.1 = (f32[8,128]{1,0:T(8,128)S(1)}, f32[8,128]{1,0:T(8,128)}, u32[]{:S(2)}) copy-start(f32[8,128]{1,0:T(8,128)} %residual.1) | copy-start | bytes 12292
  20.1 16.7 %copy-start.2 = (f32[128]{0:T(128)S(1)}, f32[128]{0:T(128)}, u32[]{:S(2)}) copy-start(f32[128]{0:T(128)} %param.21) | copy-start | bytes 1540
  20.1 33.7 %slice-start = ((s8[6815744]{0:T(1024)(128)(4,1)}), s8[4194304]{0:T(1024)(128)(4,1)S(1)}, s32[]{:S(2)}) async-start(s8[6815744]{0:T(1024)(128)(4,1)} %bitcast.2), calls=%async_computation.4 | async-start | bytes 8388608
  20.1 33.7 %slice-start.2 = ((s8[6815744]{0:T(1024)(128)(4,1)}), s8[4194304]{0:T(1024)(128)(4,1)S(1)}, s32[]{:S(2)}) async-start(s8[6815744]{0:T(1024)(128)(4,1)} %bitcast.4), calls=%async_computation.6 | async-start | bytes 8388608
  20.1 33.6 %slice-start.4 = ((s8[6815744]{0:T(1024)(128)(4,1)}), s8[4194304]{0:T(1024)(128)(4,1)S(1)}, s32[]{:S(2)}) async-start(s8[6815744]{0:T(1024)(128)(4,1)} %bitcast.6), calls=%async_computation.8 | async-start | bytes 8388608
  36.8 17.0 %slice-start.1 = ((s8[6815744]{0:T(1024)(128)(4,1)}), s8[2621440]{0:T(1024)(128)(4,1)S(1)}, s32[]{:S(2)}) async-start(s8[6815744]{0:T(1024)(128)(4,1)} %bitcast.2), calls=%async_computation.5 | async-start | bytes 5242880
  36.8 17.0 %slice-start.3 = ((s8[6815744]{0:T(1024)(128)(4,1)}), s8[2621440]{0:T(1024)(128)(4,1)S(1)}, s32[]{:S(2)}) async-start(s8[6815744]{0:T(1024)(128)(4,1)} %bitcast.4), calls=%async_computation.7 | async-start | bytes 5242880
  36.8 17.0 %slice-start.5 = ((s8[6815744]{0:T(1024)(128)(4,1)}), s8[2621440]{0:T(1024)(128)(4,1)S(1)}, s32[]{:S(2)}) async-start(s8[6815744]{0:T(1024)(128)(4,1)} %bitcast.6), calls=%async_computation.9 | async-start | bytes 5242880

commit v3 on v2

--- a/solution.py
+++ b/solution.py
@@ -14,6 +14,7 @@
 ANY = pl.BlockSpec(memory_space=pl.ANY)
 MIB = 1 << 20
 CHUNK = 2048
+STEP = 256
 COST = pl.CostEstimate(flops=20 * 10**9, bytes_accessed=60 * 10**6, transcendentals=20 * 10**6)
 
 
@@ -65,13 +66,11 @@
     new_keys_hbm,
     new_values_hbm,
     payload,
-    keys_out,
-    values_out,
+    keys,
+    values,
     new_block,
     fill,
     queries,
-    keys,
-    values,
     new_keys,
     new_values,
     rows_f32,
@@ -95,7 +94,6 @@
     )
     wait_copies(copies)
     place_rows(block, new_block, fill, ((new_keys, keys), (new_values, values)))
-    writes = start_copies(((keys, keys_out), (values, values_out)), sems, len(copies))
 
     lane = lax.broadcasted_iota(jnp.int32, (group, rows), 1)
     places = [(b, k) for b in range(batch) for k in range(kv_local)]
@@ -115,7 +113,6 @@
         rows_f32[pl.ds(base, group, stride=16), :] = summed
         rows_f32[pl.ds(base + 8, group, stride=16), :] = stats
     payload[...] = rows_f32[...].reshape(heads_local, 16, head_dim).astype(BF16)
-    wait_copies(writes)
 
 
 def combine_kernel(parts, out):
@@ -156,29 +153,35 @@
             payload[p, j] = pair
 
 
-def feed_kernel(tiles, gate, up, down, out):
+def feed_kernel(tiles, gate, up, down, keys, values, out, keys_out, values_out, sems):
+    writes = start_copies(((keys, keys_out), (values, values_out)), sems)
     features = gate.shape[1]
-    chunks = features // CHUNK
-    per = CHUNK // 128
     squares = tree_sum(tiles[p, 4].astype(F32) for p in range(tiles.shape[0]))
     squares = squares + pltpu.roll(squares, 64, 1)
     factor = jnp.concatenate([lax.rsqrt(squares[0:1, b : b + 1] / features + 1e-05) for b in range(8)], axis=0)
     gate_sum = 0.0
     up_sum = 0.0
-    for c in range(chunks):
+    for c in range(features // STEP):
+        first = c * STEP // 128
         piece = jnp.concatenate(
-            [jnp.concatenate([tiles[c * per + i, j] for j in range(4)], axis=0) for i in range(per)], axis=1
+            [
+                jnp.concatenate([tiles[first + i, j] for j in range(tiles.shape[1] - 1)], axis=0)
+                for i in range(STEP // 128)
+            ],
+            axis=1,
         )
-        part = slice(c * CHUNK, (c + 1) * CHUNK)
+        part = slice(c * STEP, (c + 1) * STEP)
         gate_sum = gate_sum + nt_dot(gate[:, part], piece)
-        up_sum = up_sum + nt_dot(up[:, part], piece)
+        up_sum = up_sum + nt_dot(piece, up[:, part])
     gate_sum = gate_sum.T * factor
-    up_sum = up_sum.T * factor
+    up_sum = up_sum * factor
     hidden = (gate_sum / (1.0 + jnp.exp(-gate_sum)) * up_sum).astype(BF16)
-    for c in range(chunks):
+    per = CHUNK // 128
+    for c in range(features // CHUNK):
         sums = jnp.dot(hidden, down[:, c * CHUNK : (c + 1) * CHUNK], preferred_element_type=F32).astype(BF16)
         for i in range(per):
             out[c * per + i] = sums[:, i * 128 : (i + 1) * 128]
+    wait_copies(writes)
 
 
 def finish_kernel(sums, mixed, out):
@@ -223,27 +226,25 @@
     columns = residual.shape[1]
     fill = block_fill.reshape(batch)
     counts = [pltpu.SMEM((batch,), jnp.int32)] * 2
-    caches = [pltpu.VMEM(key_cache.shape, BF16)] * 2
     fresh = [pltpu.VMEM(new_keys.shape, BF16)] * 2
 
-    partials, keys_out, values_out = call(
+    partials, held_keys, held_values = call(
         attention_kernel,
         "attention",
         [*map(in_hbm, (new_block, fill, queries, key_cache, value_cache, new_keys, new_values))],
         [ANY] * 7,
         (
             jax.ShapeDtypeStruct((heads_local, 16, head_dim), BF16),
-            jax.ShapeDtypeStruct(key_cache.shape, BF16),
-            jax.ShapeDtypeStruct(value_cache.shape, BF16),
-        ),
-        (VMEM, ANY, ANY),
+            pltpu.VMEM(key_cache.shape, BF16),
+            pltpu.VMEM(value_cache.shape, BF16),
+        ),
+        (VMEM, VMEM, VMEM),
         [
             *counts,
             pltpu.VMEM(queries.shape, BF16),
-            *caches,
             *fresh,
             pltpu.VMEM((heads_local * 16, head_dim), F32),
-            pltpu.SemaphoreType.DMA((9,)),
+            pltpu.SemaphoreType.DMA((7,)),
         ],
     )
     gathered = lax.all_to_all(partials, "seq", 0, 0)
@@ -268,13 +269,18 @@
         (VMEM, VMEM),
     )
     all_stream = lax.all_to_all(stream, EVERY, 0, 0)
-    sums = call(
+    sums, keys_out, values_out = call(
         feed_kernel,
         "feed",
-        [all_stream, gate_weight, up_weight, down_weight],
-        [VMEM] * 4,
-        jax.ShapeDtypeStruct((devices, batch, columns), BF16),
-        VMEM,
+        [all_stream, gate_weight, up_weight, down_weight, held_keys, held_values],
+        [VMEM] * 6,
+        (
+            jax.ShapeDtypeStruct((devices, batch, columns), BF16),
+            jax.ShapeDtypeStruct(key_cache.shape, BF16),
+            jax.ShapeDtypeStruct(value_cache.shape, BF16),
+        ),
+        (VMEM, ANY, ANY),
+        [pltpu.SemaphoreType.DMA((2,))],
     )
     all_sums = lax.all_to_all(sums, EVERY, 0, 0)
     layer_out = call(

time: 74.7 us -> 72.9 us (0.976)
  Pallas kernels: 8.84 us -> 6.98 us
    pallas_call x5, Pallas kernels: 8.84 us -> 6.98 us  [call(): pl.pallas_call(kernel, out_shape=out_shape, in_specs=in_specs, out_specs=...]
where the time goes in v3:
time: 72.9 us; the launch traced here: 72.7 us
  blocking collectives  64.9 us (89%)
  Pallas kernels  6.98 us (10%)
  between operations  0.77 us (1%)
    all_to_all x1, blocking collectives, body(): gathered = lax.all_to_all(partials, 'seq', 0, 0)  17.1 us
    all_to_all x1, blocking collectives, body(): all_heads = lax.all_to_all(heads, EVERY, 0, 0)  16.4 us
    all_to_all x1, blocking collectives, body(): all_stream = lax.all_to_all(stream, EVERY, 0, 0)  16 us
    all_to_all x1, blocking collectives, body(): all_sums = lax.all_to_all(sums, EVERY, 0, 0)  15.4 us
    pallas_call x5, Pallas kernels, call(): pl.pallas_call(kernel, out_shape=out_shape, in_specs=in_specs, out_specs=...  6.98 us

profile of v3, /device:TPU:1, one launch (start us, length us, event | category | flops | bytes accessed | tf_op | source)
XLA Modules:
  0.0 72.7 jit_solution(9395282759330062050)
XLA Ops:
  0.6 2.0 %attention.1 = (bf16[32,16,128]{2,1,0:T(8,128)(2,1)S(1)}, bf16[8,2,128,128]{3,2,1,0:T(8,128)(2,1)S(1)}, bf16[8,2,128,128]{3,2,1,0:T(8,128)(2,1)S(1)}) custom-call(s32[8]{0:T(128)} %new_block_hbm.1, s32[8]{0:T(128)} %bitcast.9, bf16[8,32,128]{2,1,0:T(8,128)(2,1)} %queries_hbm.1, bf16[8,2,128,128]{3,2,1,0:T(8,128)(2,1)} %keys_hbm.1, ...), custom_call_target="tpu_custom_call" | custom-call | flops 20000000000 | bytes 60000000 | tf_op jit(solution)/shard_map/attention/pallas_call | solution.py:197
  2.6 17.1 %all_to_all.20.parts = bf16[32,16,128]{2,1,0:T(8,128)(2,1)S(1)} all-to-all(bf16[32,16,128]{2,1,0:T(8,128)(2,1)S(1)} %get-tuple-element.11), channel_id=1, replica_groups=mesh['kvh'=4,'seq'=32] {'seq'}, dimensions={0} | all-to-all | bytes 262144 | tf_op jit(solution)/shard_map/all_to_all | solution.py:250
  19.7 0.0 copy-start
  19.7 0.0 copy-start.1
  19.7 0.0 copy-start.2
  19.7 0.0 slice-start
  19.7 0.0 slice-start.2
  19.7 0.0 slice-start.4
  19.8 0.2 combine.1
  20.0 16.4 %all_to_all.21.heads = bf16[128,8,128]{2,1,0:T(8,128)(2,1)S(1)} all-to-all(bf16[128,8,128]{2,1,0:T(8,128)(2,1)S(1)} %combine.1), channel_id=1, replica_groups=mesh['kvh'=4,'seq'=32] {'kvh','seq'}, dimensions={0} | all-to-all | bytes 524288 | tf_op jit(solution)/shard_map/all_to_all | solution.py:259
  36.4 0.0 copy-done
  36.4 0.0 copy-done.1
  36.4 0.0 copy-done.2
  36.4 0.0 slice-start.1
  36.4 0.0 slice-start.3
  36.4 0.0 slice-start.5
  36.5 0.9 %project.1 = (f32[8,128]{1,0:T(8,128)S(1)}, bf16[128,5,2,128]{3,2,1,0:T(2,128)(2,1)S(1)}) custom-call(bf16[128,8,128]{2,1,0:T(8,128)(2,1)S(1)} %all_to_all.21.heads, f32[8,128]{1,0:T(8,128)S(1)} %copy-done.1, f32[1,128]{1,0:T(1,128)S(1)} %bitcast.8, bf16[16384,128]{1,0:T(8,128)(2,1)S(1)} %copy-done), custom_call_target="tpu_custom_call" | custom-call | flops 20000000000 | bytes 60000000 | tf_op jit(solution)/shard_map/project/pallas_call | solution.py:197
  37.4 16.0 %all_to_all.22.tiles = bf16[128,5,2,128]{3,2,1,0:T(2,128)(2,1)S(1)} all-to-all(bf16[128,5,2,128]{3,2,1,0:T(2,128)(2,1)S(1)} %get-tuple-element.12), channel_id=1, replica_groups=mesh['kvh'=4,'seq'=32] {'kvh','seq'}, dimensions={0} | all-to-all | bytes 655360 | tf_op jit(solution)/shard_map/all_to_all | solution.py:271
  53.4 0.0 slice-done
  53.4 0.0 slice-done.2
  53.4 0.0 slice-done.4
  53.4 0.0 slice-done.1
  53.4 0.0 slice-done.3
  53.4 0.0 slice-done.5
  53.4 3.2 %feed.1 = (bf16[128,8,128]{2,1,0:T(8,128)(2,1)S(1)}, bf16[8,2,128,128]{3,2,1,0:T(8,128)(2,1)}, bf16[8,2,128,128]{3,2,1,0:T(8,128)(2,1)}) custom-call(bf16[128,5,2,128]{3,2,1,0:T(2,128)(2,1)S(1)} %all_to_all.22.tiles, bf16[208,16384]{1,0:T(8,128)(2,1)S(1)} %bitcast.3, bf16[208,16384]{1,0:T(8,128)(2,1)S(1)} %bitcast.5, bf16[208,16384]{1,0:T(8,128)(2,1)S(1)} %bitcast.7, ...), custom_call_target="tpu_custom_call" | custom-call | flops 20000000000 | bytes 60000000 | tf_op jit(solution)/shard_map/feed/pallas_call | solution.py:197
  56.7 15.4 %all_to_all.23.sums = bf16[128,8,128]{2,1,0:T(8,128)(2,1)S(1)} all-to-all(bf16[128,8,128]{2,1,0:T(8,128)(2,1)S(1)} %get-tuple-element.15), channel_id=1, replica_groups=mesh['kvh'=4,'seq'=32] {'kvh','seq'}, dimensions={0} | all-to-all | bytes 524288 | tf_op jit(solution)/shard_map/all_to_all | solution.py:285
  72.1 0.6 finish.1
  (3 shorter events, 0.0 us)
Async XLA Ops:
  19.7 16.7 %copy-start = (bf16[16384,128]{1,0:T(8,128)(2,1)S(1)}, bf16[16384,128]{1,0:T(8,128)(2,1)}, u32[]{:S(2)}) copy-start(bf16[16384,128]{1,0:T(8,128)(2,1)} %weight.1) | copy-start | bytes 12582916
  19.7 16.7 %copy-start.1 = (f32[8,128]{1,0:T(8,128)S(1)}, f32[8,128]{1,0:T(8,128)}, u32[]{:S(2)}) copy-start(f32[8,128]{1,0:T(8,128)} %residual.1) | copy-start | bytes 12292
  19.7 16.7 %copy-start.2 = (f32[128]{0:T(128)S(1)}, f32[128]{0:T(128)}, u32[]{:S(2)}) copy-start(f32[128]{0:T(128)} %param.21) | copy-start | bytes 1540
  19.7 33.7 %slice-start = ((s8[6815744]{0:T(1024)(128)(4,1)}), s8[4194304]{0:T(1024)(128)(4,1)S(1)}, s32[]{:S(2)}) async-start(s8[6815744]{0:T(1024)(128)(4,1)} %bitcast.2), calls=%async_computation.4 | async-start | bytes 8388608
  19.7 33.7 %slice-start.2 = ((s8[6815744]{0:T(1024)(128)(4,1)}), s8[4194304]{0:T(1024)(128)(4,1)S(1)}, s32[]{:S(2)}) async-start(s8[6815744]{0:T(1024)(128)(4,1)} %bitcast.4), calls=%async_computation.6 | async-start | bytes 8388608
  19.7 33.6 %slice-start.4 = ((s8[6815744]{0:T(1024)(128)(4,1)}), s8[4194304]{0:T(1024)(128)(4,1)S(1)}, s32[]{:S(2)}) async-start(s8[6815744]{0:T(1024)(128)(4,1)} %bitcast.6), calls=%async_computation.8 | async-start | bytes 8388608
  36.4 17.0 %slice-start.1 = ((s8[6815744]{0:T(1024)(128)(4,1)}), s8[2621440]{0:T(1024)(128)(4,1)S(1)}, s32[]{:S(2)}) async-start(s8[6815744]{0:T(1024)(128)(4,1)} %bitcast.2), calls=%async_computation.5 | async-start | bytes 5242880
  36.4 17.0 %slice-start.3 = ((s8[6815744]{0:T(1024)(128)(4,1)}), s8[2621440]{0:T(1024)(128)(4,1)S(1)}, s32[]{:S(2)}) async-start(s8[6815744]{0:T(1024)(128)(4,1)} %bitcast.4), calls=%async_computation.7 | async-start | bytes 5242880
  36.4 17.0 %slice-start.5 = ((s8[6815744]{0:T(1024)(128)(4,1)}), s8[2621440]{0:T(1024)(128)(4,1)S(1)}, s32[]{:S(2)}) async-start(s8[6815744]{0:T(1024)(128)(4,1)} %bitcast.6), calls=%async_computation.9 | async-start | bytes 5242880

commit v4 on v3

--- a/solution.py
+++ b/solution.py
@@ -42,19 +42,21 @@
         copy.wait()
 
 
-def place_rows(block, new_block, fill, caches):
-    batch, kv_local, _, head_dim = caches[0][1].shape
+def place_row(block, new_block, fill, new, cache):
+    batch, kv_local, _, head_dim = cache.shape
+    request = jnp.int32(-1)
     for b in range(batch):
-
-        @pl.when(new_block[b] == block)
-        def _():
-            start = pl.multiple_of((fill[b] // 16) * 16, 16)
-            hit = lax.broadcasted_iota(jnp.int32, (16, head_dim), 0) == fill[b] - start
-            for k in range(kv_local):
-                for new, cache in caches:
-                    old = cache[b, k, pl.ds(start, 16), :].astype(F32)
-                    row = new[b, k : k + 1, :].astype(F32)
-                    cache[b, k, pl.ds(start, 16), :] = jnp.where(hit, row, old).astype(BF16)
+        request = jnp.where(new_block[b] == block, b, request)
+
+    @pl.when(request >= 0)
+    def _():
+        row = fill[request]
+        start = pl.multiple_of((row // 16) * 16, 16)
+        hit = lax.broadcasted_iota(jnp.int32, (16, head_dim), 0) == row - start
+        for k in range(kv_local):
+            old = cache[request, k, pl.ds(start, 16), :].astype(F32)
+            fresh = new[request, k : k + 1, :].astype(F32)
+            cache[request, k, pl.ds(start, 16), :] = jnp.where(hit, fresh, old).astype(BF16)
 
 
 def attention_kernel(
@@ -83,17 +85,17 @@
     copies = start_copies(
         (
             (keys_hbm, keys),
-            (values_hbm, values),
             (queries_hbm, queries),
             (new_keys_hbm, new_keys),
-            (new_values_hbm, new_values),
             (new_block_hbm, new_block),
             (fill_hbm, fill),
+            (values_hbm, values),
+            (new_values_hbm, new_values),
         ),
         sems,
     )
-    wait_copies(copies)
-    place_rows(block, new_block, fill, ((new_keys, keys), (new_values, values)))
+    wait_copies(copies[:5])
+    place_row(block, new_block, fill, new_keys, keys)
 
     lane = lax.broadcasted_iota(jnp.int32, (group, rows), 1)
     places = [(b, k) for b in range(batch) for k in range(kv_local)]
@@ -104,26 +106,43 @@
     weights = [
         jnp.where(live[b], jnp.exp(s - t), 0.0).astype(BF16) for (b, _), s, t in zip(places, scores, tops)
     ]
+    totals = [jnp.sum(w.astype(F32), axis=1, keepdims=True) for w in weights]
+    wait_copies(copies[5:])
+    place_row(block, new_block, fill, new_values, values)
     sums = [jnp.dot(w, values[b, k], preferred_element_type=F32) for (b, k), w in zip(places, weights)]
-    totals = [jnp.sum(w.astype(F32), axis=1, keepdims=True) for w in weights]
-    for (b, k), top, total, summed in zip(places, tops, totals, sums):
-        high = total.astype(BF16).astype(F32)
-        stats = jnp.where(lane < 32, top, jnp.where(lane < 64, high, total - high))
-        base = k * group * 16 + b
-        rows_f32[pl.ds(base, group, stride=16), :] = summed
-        rows_f32[pl.ds(base + 8, group, stride=16), :] = stats
-    payload[...] = rows_f32[...].reshape(heads_local, 16, head_dim).astype(BF16)
-
-
-def combine_kernel(parts, out):
-    sources = parts.shape[0]
-    tiles = [parts[s].astype(F32) for s in range(sources)]
-    stats = [t[8:16] for t in tiles]
-    top = functools.reduce(jnp.maximum, stats)
-    weights = [jnp.exp(jnp.minimum(s - top, 0.0)) for s in stats]
-    total = tree_sum(w * (pltpu.roll(s, 96, 1) + pltpu.roll(s, 64, 1)) for s, w in zip(stats, weights))
-    scale = 1.0 / total
-    heads = tree_sum(t[0:8] * (w * scale)[:, 0:1] for t, w in zip(tiles, weights)).astype(BF16)
+    height = batch + 2
+    for (b, k), summed in zip(places, sums):
+        rows_f32[pl.ds(k * group * height + b, group, stride=height), :] = summed
+    for k in range(kv_local):
+        first = jnp.zeros(lane.shape, F32)
+        second = jnp.zeros(lane.shape, F32)
+        for b in range(batch):
+            top, total = tops[b * kv_local + k], totals[b * kv_local + k]
+            high = total.astype(BF16).astype(F32)
+            first = jnp.where(lane == b, top, jnp.where(lane == 64 + b, high, first))
+            second = jnp.where(lane == b, total - high, second)
+        rows_f32[pl.ds(k * group * height + batch, group, stride=height), :] = first
+        rows_f32[pl.ds(k * group * height + batch + 1, group, stride=height), :] = second
+    payload[...] = rows_f32[...].astype(BF16)
+
+
+def combine_kernel(parts, out, rows):
+    batch = out.shape[1]
+    height = batch + 2
+    sources = parts.shape[0] // height
+    rows[...] = parts[...].astype(F32)
+    first = rows[pl.ds(batch, sources, stride=height), :]
+    second = rows[pl.ds(batch + 1, sources, stride=height), :]
+    total = pltpu.roll(first, 64, 1) + second
+    weights = jnp.exp(jnp.minimum(first - jnp.max(first, axis=0, keepdims=True), 0.0))
+    scale = weights / jnp.sum(weights * total, axis=0, keepdims=True)
+    heads = jnp.concatenate(
+        [
+            jnp.sum(rows[pl.ds(b, sources, stride=height), :] * scale[:, b : b + 1], axis=0, keepdims=True)
+            for b in range(batch)
+        ],
+        axis=0,
+    ).astype(BF16)
     for p in range(out.shape[0]):
         out[p] = heads
 
@@ -147,10 +166,9 @@
     for b in range(total.shape[0]):
         stats = jnp.where(lane == b, high[b : b + 1], jnp.where(lane == 64 + b, low[b : b + 1], stats))
     tile = jnp.concatenate([total * gain[...], stats], axis=0).astype(BF16)
-    for j in range(payload.shape[1]):
-        pair = tile[2 * j : 2 * j + 2]
-        for p in range(payload.shape[0]):
-            payload[p, j] = pair
+    whole = jnp.concatenate([tile] * (payload.shape[1] // tile.shape[0]), axis=0)
+    for p in range(payload.shape[0]):
+        payload[p] = whole
 
 
 def feed_kernel(tiles, gate, up, down, keys, values, out, keys_out, values_out, sems):
@@ -234,7 +252,7 @@
         [*map(in_hbm, (new_block, fill, queries, key_cache, value_cache, new_keys, new_values))],
         [ANY] * 7,
         (
-            jax.ShapeDtypeStruct((heads_local, 16, head_dim), BF16),
+            jax.ShapeDtypeStruct((heads_local * (batch + 2), head_dim), BF16),
             pltpu.VMEM(key_cache.shape, BF16),
             pltpu.VMEM(value_cache.shape, BF16),
         ),
@@ -243,11 +261,12 @@
             *counts,
             pltpu.VMEM(queries.shape, BF16),
             *fresh,
-            pltpu.VMEM((heads_local * 16, head_dim), F32),
+            pltpu.VMEM((heads_local * (batch + 2), head_dim), F32),
             pltpu.SemaphoreType.DMA((7,)),
         ],
     )
-    gathered = lax.all_to_all(partials, "seq", 0, 0)
+    partials = partials.reshape(heads_local, batch // 2 + 1, 2, head_dim)
+    gathered = lax.all_to_all(partials, "seq", 0, 0).reshape(heads_local * (batch + 2), head_dim)
     heads = call(
         combine_kernel,
         "combine",
@@ -255,6 +274,7 @@
         [VMEM],
         jax.ShapeDtypeStruct((devices, batch, head_dim), BF16),
         VMEM,
+        [pltpu.VMEM((heads_local * (batch + 2), head_dim), F32)],
     )
     all_heads = lax.all_to_all(heads, EVERY, 0, 0)
     mixed, stream = call(
@@ -264,10 +284,11 @@
         [VMEM] * 4,
         (
             jax.ShapeDtypeStruct((batch, columns), F32),
-            jax.ShapeDtypeStruct((devices, batch // 2 + 1, 2, columns), BF16),
+            jax.ShapeDtypeStruct((devices // 8, 8 * (batch + 2), columns), BF16),
         ),
         (VMEM, VMEM),
     )
+    stream = stream.reshape(devices, batch // 2 + 1, 2, columns)
     all_stream = lax.all_to_all(stream, EVERY, 0, 0)
     sums, keys_out, values_out = call(
         feed_kernel,

time: 72.9 us -> 72.4 us (level)
  no operation moved by 1% of the time
where the time goes in v4:
time: 72.4 us; the launch traced here: 72.2 us
  blocking collectives  64.5 us (89%)
  Pallas kernels  6.88 us (10%)
  between operations  0.77 us (1%)
    all_to_all x1, blocking collectives, body(): lax.all_to_all(partials, 'seq', 0, 0)  16.8 us
    all_to_all x1, blocking collectives, body(): all_heads = lax.all_to_all(heads, EVERY, 0, 0)  16.3 us
    all_to_all x1, blocking collectives, body(): all_stream = lax.all_to_all(stream, EVERY, 0, 0)  16 us
    all_to_all x1, blocking collectives, body(): all_sums = lax.all_to_all(sums, EVERY, 0, 0)  15.4 us
    pallas_call x5, Pallas kernels, call(): pl.pallas_call(kernel, out_shape=out_shape, in_specs=in_specs, out_specs=...  6.88 us

profile of v4, /device:TPU:1, one launch (start us, length us, event | category | flops | bytes accessed | tf_op | source)
XLA Modules:
  0.0 72.2 jit_solution(8744586911787729724)
XLA Ops:
  0.6 2.0 %attention.1 = (bf16[320,128]{1,0:T(8,128)(2,1)S(1)}, bf16[8,2,128,128]{3,2,1,0:T(8,128)(2,1)S(1)}, bf16[8,2,128,128]{3,2,1,0:T(8,128)(2,1)S(1)}) custom-call(s32[8]{0:T(128)} %new_block_hbm.1, s32[8]{0:T(128)} %bitcast.15, bf16[8,32,128]{2,1,0:T(8,128)(2,1)} %queries_hbm.1, bf16[8,2,128,128]{3,2,1,0:T(8,128)(2,1)} %keys_hbm.1, ...), custom_call_target="tpu_custom_call" | custom-call | flops 20000000000 | bytes 60000000 | tf_op jit(solution)/shard_map/attention/pallas_call | solution.py:215
  2.6 16.8 %all_to_all.20 = bf16[32,5,2,128]{3,2,1,0:T(2,128)(2,1)S(1)} all-to-all(bf16[32,5,2,128]{3,2,1,0:T(2,128)(2,1)S(1)} %bitcast.6), channel_id=1, replica_groups=mesh['kvh'=4,'seq'=32] {'seq'}, dimensions={0} | all-to-all | bytes 163840 | tf_op jit(solution)/shard_map/all_to_all | solution.py:269
  19.4 0.0 copy-start
  19.4 0.0 copy-start.1
  19.4 0.0 copy-start.2
  19.4 0.0 slice-start
  19.4 0.0 slice-start.2
  19.4 0.0 slice-start.4
  19.5 0.2 combine.1
  19.7 16.3 %all_to_all.21.heads = bf16[128,8,128]{2,1,0:T(8,128)(2,1)S(1)} all-to-all(bf16[128,8,128]{2,1,0:T(8,128)(2,1)S(1)} %combine.1), channel_id=1, replica_groups=mesh['kvh'=4,'seq'=32] {'kvh','seq'}, dimensions={0} | all-to-all | bytes 524288 | tf_op jit(solution)/shard_map/all_to_all | solution.py:279
  36.1 0.0 copy-done
  36.1 0.0 copy-done.1
  36.1 0.0 copy-done.2
  36.1 0.0 slice-start.1
  36.1 0.0 slice-start.3
  36.1 0.0 slice-start.5
  36.1 0.8 %project.1 = (f32[8,128]{1,0:T(8,128)S(1)}, bf16[16,80,128]{2,1,0:T(8,128)(2,1)S(1)}) custom-call(bf16[128,8,128]{2,1,0:T(8,128)(2,1)S(1)} %all_to_all.21.heads, f32[8,128]{1,0:T(8,128)S(1)} %copy-done.1, f32[1,128]{1,0:T(1,128)S(1)} %bitcast.14, bf16[16384,128]{1,0:T(8,128)(2,1)S(1)} %copy-done), custom_call_target="tpu_custom_call" | custom-call | flops 20000000000 | bytes 60000000 | tf_op jit(solution)/shard_map/project/pallas_call | solution.py:215
  36.9 16.0 %all_to_all.22.tiles = bf16[128,5,2,128]{3,2,1,0:T(2,128)(2,1)S(1)} all-to-all(bf16[128,5,2,128]{3,2,1,0:T(2,128)(2,1)S(1)} %bitcast.5), channel_id=1, replica_groups=mesh['kvh'=4,'seq'=32] {'kvh','seq'}, dimensions={0} | all-to-all | bytes 655360 | tf_op jit(solution)/shard_map/all_to_all | solution.py:292
  52.9 0.0 slice-done
  52.9 0.0 slice-done.2
  52.9 0.0 slice-done.4
  52.9 0.0 slice-done.1
  52.9 0.0 slice-done.3
  52.9 0.0 slice-done.5
  53.0 3.2 %feed.1 = (bf16[128,8,128]{2,1,0:T(8,128)(2,1)S(1)}, bf16[8,2,128,128]{3,2,1,0:T(8,128)(2,1)}, bf16[8,2,128,128]{3,2,1,0:T(8,128)(2,1)}) custom-call(bf16[128,5,2,128]{3,2,1,0:T(2,128)(2,1)S(1)} %all_to_all.22.tiles, bf16[208,16384]{1,0:T(8,128)(2,1)S(1)} %bitcast.9, bf16[208,16384]{1,0:T(8,128)(2,1)S(1)} %bitcast.11, bf16[208,16384]{1,0:T(8,128)(2,1)S(1)} %bitcast.13, ...), custom_call_target="tpu_custom_call" | custom-call | flops 20000000000 | bytes 60000000 | tf_op jit(solution)/shard_map/feed/pallas_call | solution.py:215
  56.2 15.4 %all_to_all.23.sums = bf16[128,8,128]{2,1,0:T(8,128)(2,1)S(1)} all-to-all(bf16[128,8,128]{2,1,0:T(8,128)(2,1)S(1)} %get-tuple-element.15), channel_id=1, replica_groups=mesh['kvh'=4,'seq'=32] {'kvh','seq'}, dimensions={0} | all-to-all | bytes 524288 | tf_op jit(solution)/shard_map/all_to_all | solution.py:306
  71.6 0.6 finish.1
  (3 shorter events, 0.0 us)
Async XLA Ops:
  19.4 16.6 %copy-start = (bf16[16384,128]{1,0:T(8,128)(2,1)S(1)}, bf16[16384,128]{1,0:T(8,128)(2,1)}, u32[]{:S(2)}) copy-start(bf16[16384,128]{1,0:T(8,128)(2,1)} %weight.1) | copy-start | bytes 12582916
  19.4 16.6 %copy-start.1 = (f32[8,128]{1,0:T(8,128)S(1)}, f32[8,128]{1,0:T(8,128)}, u32[]{:S(2)}) copy-start(f32[8,128]{1,0:T(8,128)} %residual.1) | copy-start | bytes 12292
  19.4 16.6 %copy-start.2 = (f32[128]{0:T(128)S(1)}, f32[128]{0:T(128)}, u32[]{:S(2)}) copy-start(f32[128]{0:T(128)} %param.21) | copy-start | bytes 1540
  19.4 33.5 %slice-start = ((s8[6815744]{0:T(1024)(128)(4,1)}), s8[4194304]{0:T(1024)(128)(4,1)S(1)}, s32[]{:S(2)}) async-start(s8[6815744]{0:T(1024)(128)(4,1)} %bitcast.8), calls=%async_computation.4 | async-start | bytes 8388608
  19.4 33.5 %slice-start.2 = ((s8[6815744]{0:T(1024)(128)(4,1)}), s8[4194304]{0:T(1024)(128)(4,1)S(1)}, s32[]{:S(2)}) async-start(s8[6815744]{0:T(1024)(128)(4,1)} %bitcast.10), calls=%async_computation.6 | async-start | bytes 8388608
  19.4 33.5 %slice-start.4 = ((s8[6815744]{0:T(1024)(128)(4,1)}), s8[4194304]{0:T(1024)(128)(4,1)S(1)}, s32[]{:S(2)}) async-start(s8[6815744]{0:T(1024)(128)(4,1)} %bitcast.12), calls=%async_computation.8 | async-start | bytes 8388608
  36.1 16.9 %slice-start.1 = ((s8[6815744]{0:T(1024)(128)(4,1)}), s8[2621440]{0:T(1024)(128)(4,1)S(1)}, s32[]{:S(2)}) async-start(s8[6815744]{0:T(1024)(128)(4,1)} %bitcast.8), calls=%async_computation.5 | async-start | bytes 5242880
  36.1 16.9 %slice-start.3 = ((s8[6815744]{0:T(1024)(128)(4,1)}), s8[2621440]{0:T(1024)(128)(4,1)S(1)}, s32[]{:S(2)}) async-start(s8[6815744]{0:T(1024)(128)(4,1)} %bitcast.10), calls=%async_computation.7 | async-start | bytes 5242880
  36.1 16.9 %slice-start.5 = ((s8[6815744]{0:T(1024)(128)(4,1)}), s8[2621440]{0:T(1024)(128)(4,1)S(1)}, s32[]{:S(2)}) async-start(s8[6815744]{0:T(1024)(128)(4,1)} %bitcast.12), calls=%async_computation.9 | async-start | bytes 5242880

commit v5 on v4

--- a/solution.py
+++ b/solution.py
@@ -2,6 +2,7 @@
 
 import jax
 import jax.numpy as jnp
+import numpy as np
 from jax import lax
 from jax.experimental import pallas as pl
 from jax.experimental.pallas import tpu as pltpu
@@ -9,7 +10,11 @@
 
 F32 = jnp.float32
 BF16 = jnp.bfloat16
-EVERY = ("kvh", "seq")
+SEQ = ("y", "z", "core")
+EVERY = ("kvh", "y", "z", "core")
+SIZES = (4, 4, 4, 2)
+ORDER = ("core", "z", "y", "kvh")
+SLOT = np.arange(128).reshape(SIZES).transpose([EVERY.index(axis) for axis in ORDER]).reshape(-1).argsort().tolist()
 VMEM = pl.BlockSpec(memory_space=pltpu.VMEM)
 ANY = pl.BlockSpec(memory_space=pl.ANY)
 MIB = 1 << 20
@@ -81,7 +86,7 @@
     batch, heads_local, head_dim = queries.shape
     kv_local, rows = keys.shape[1], keys.shape[2]
     group = heads_local // kv_local
-    block = lax.axis_index("seq")
+    block = (lax.axis_index("y") * lax.axis_size("z") + lax.axis_index("z")) * 2 + lax.axis_index("core")
     copies = start_copies(
         (
             (keys_hbm, keys),
@@ -151,7 +156,7 @@
     per = CHUNK // 128
     total = residual[...] + tree_sum(
         jnp.dot(
-            jnp.concatenate([heads[c * per + i] for i in range(per)], axis=1),
+            jnp.concatenate([heads[SLOT[c * per + i]] for i in range(per)], axis=1),
             weight[c * CHUNK : (c + 1) * CHUNK, :],
             preferred_element_type=F32,
         )
@@ -183,7 +188,7 @@
         first = c * STEP // 128
         piece = jnp.concatenate(
             [
-                jnp.concatenate([tiles[first + i, j] for j in range(tiles.shape[1] - 1)], axis=0)
+                jnp.concatenate([tiles[SLOT[first + i], j] for j in range(tiles.shape[1] - 1)], axis=0)
                 for i in range(STEP // 128)
             ],
             axis=1,
@@ -198,7 +203,7 @@
     for c in range(features // CHUNK):
         sums = jnp.dot(hidden, down[:, c * CHUNK : (c + 1) * CHUNK], preferred_element_type=F32).astype(BF16)
         for i in range(per):
-            out[c * per + i] = sums[:, i * 128 : (i + 1) * 128]
+            out[SLOT[c * per + i]] = sums[:, i * 128 : (i + 1) * 128]
     wait_copies(writes)
 
 
@@ -240,7 +245,7 @@
     down_weight,
 ):
     batch, heads_local, head_dim = queries.shape
-    devices = lax.axis_size("kvh") * lax.axis_size("seq")
+    devices = lax.axis_size(EVERY)
     columns = residual.shape[1]
     fill = block_fill.reshape(batch)
     counts = [pltpu.SMEM((batch,), jnp.int32)] * 2
@@ -266,7 +271,7 @@
         ],
     )
     partials = partials.reshape(heads_local, batch // 2 + 1, 2, head_dim)
-    gathered = lax.all_to_all(partials, "seq", 0, 0).reshape(heads_local * (batch + 2), head_dim)
+    gathered = lax.all_to_all(partials, SEQ, 0, 0).reshape(heads_local * (batch + 2), head_dim)
     heads = call(
         combine_kernel,
         "combine",
@@ -276,7 +281,7 @@
         VMEM,
         [pltpu.VMEM((heads_local * (batch + 2), head_dim), F32)],
     )
-    all_heads = lax.all_to_all(heads, EVERY, 0, 0)
+    all_heads = lax.all_to_all(heads, ORDER, 0, 0)
     mixed, stream = call(
         project_kernel,
         "project",
@@ -289,7 +294,7 @@
         (VMEM, VMEM),
     )
     stream = stream.reshape(devices, batch // 2 + 1, 2, columns)
-    all_stream = lax.all_to_all(stream, EVERY, 0, 0)
+    all_stream = lax.all_to_all(stream, ORDER, 0, 0)
     sums, keys_out, values_out = call(
         feed_kernel,
         "feed",
@@ -303,7 +308,7 @@
         (VMEM, ANY, ANY),
         [pltpu.SemaphoreType.DMA((2,))],
     )
-    all_sums = lax.all_to_all(sums, EVERY, 0, 0)
+    all_sums = lax.all_to_all(sums, ORDER, 0, 0)
     layer_out = call(
         finish_kernel,
         "finish",
@@ -316,29 +321,26 @@
 
 
 def solution(mesh):
+    mesh = jax.sharding.Mesh(mesh.devices.reshape(SIZES), EVERY)
     placed = (
         P(None, "kvh", None),
-        P(None, "kvh", "seq", None),
-        P(None, "kvh", "seq", None),
+        P(None, "kvh", SEQ, None),
+        P(None, "kvh", SEQ, None),
         P(None, "kvh", None),
         P(None, "kvh", None),
-        P(None, "seq"),
+        P(None, SEQ),
         P(),
-        P(None, ("kvh", "seq")),
-        P(("kvh", "seq")),
-        P(None, ("kvh", "seq")),
-        P(("kvh", "seq"), None),
-        P(("kvh", "seq"), None),
-        P(("kvh", "seq"), None),
+        P(None, EVERY),
+        P(EVERY),
+        P(None, EVERY),
+        P(EVERY, None),
+        P(EVERY, None),
+        P(EVERY, None),
     )
     return jax.shard_map(
         body,
         mesh=mesh,
         in_specs=placed,
-        out_specs=(
-            P(None, ("kvh", "seq")),
-            P(None, "kvh", "seq", None),
-            P(None, "kvh", "seq", None),
-        ),
+        out_specs=(P(None, EVERY), P(None, "kvh", SEQ, None), P(None, "kvh", SEQ, None)),
         check_vma=False,
     )

time: 72.4 us -> 71.3 us (0.985)
  blocking collectives: 64.5 us -> 63.4 us
    all_to_all x4, blocking collectives: 64.5 us -> 63.4 us  [the longest x1 16.8 us: body(): lax.all_to_all(partials, SEQ, 0, 0)]
where the time goes in v5:
time: 71.3 us; the launch traced here: 71.1 us
  blocking collectives  63.4 us (89%)
  Pallas kernels  6.85 us (10%)
  between operations  0.77 us (1%)
    all_to_all x1, blocking collectives, body(): lax.all_to_all(partials, SEQ, 0, 0)  16.8 us
    all_to_all x1, blocking collectives, body(): all_heads = lax.all_to_all(heads, ORDER, 0, 0)  16.3 us
    all_to_all x1, blocking collectives, body(): all_stream = lax.all_to_all(stream, ORDER, 0, 0)  15.5 us
    all_to_all x1, blocking collectives, body(): all_sums = lax.all_to_all(sums, ORDER, 0, 0)  14.8 us
    pallas_call x5, Pallas kernels, call(): pl.pallas_call(kernel, out_shape=out_shape, in_specs=in_specs, out_specs=...  6.85 us

profile of v5, /device:TPU:1, one launch (start us, length us, event | category | flops | bytes accessed | tf_op | source)
XLA Modules:
  0.0 71.1 jit_solution(16531224416814183594)
XLA Ops:
  0.6 2.0 %attention.1 = (bf16[320,128]{1,0:T(8,128)(2,1)S(1)}, bf16[8,2,128,128]{3,2,1,0:T(8,128)(2,1)S(1)}, bf16[8,2,128,128]{3,2,1,0:T(8,128)(2,1)S(1)}) custom-call(s32[8]{0:T(128)} %new_block_hbm.1, s32[8]{0:T(128)} %bitcast.15, bf16[8,32,128]{2,1,0:T(8,128)(2,1)} %queries_hbm.1, bf16[8,2,128,128]{3,2,1,0:T(8,128)(2,1)} %keys_hbm.1, ...), custom_call_target="tpu_custom_call" | custom-call | flops 20000000000 | bytes 60000000 | tf_op jit(solution)/shard_map/attention/pallas_call | solution.py:220
  2.6 16.8 %all_to_all.20 = bf16[32,5,2,128]{3,2,1,0:T(2,128)(2,1)S(1)} all-to-all(bf16[32,5,2,128]{3,2,1,0:T(2,128)(2,1)S(1)} %bitcast.6), channel_id=1, replica_groups=mesh['kvh'=4,'y'=4,'z'=4,'core'=2] {'y','z','core'}, dimensions={0} | all-to-all | bytes 163840 | tf_op jit(solution)/shard_map/all_to_all | solution.py:274
  19.4 0.0 copy-start
  19.4 0.0 copy-start.1
  19.4 0.0 copy-start.2
  19.4 0.0 slice-start
  19.4 0.0 slice-start.2
  19.4 0.0 slice-start.4
  19.5 0.2 combine.1
  19.7 16.3 %all_to_all.21.heads = bf16[128,8,128]{2,1,0:T(8,128)(2,1)S(1)} all-to-all(bf16[128,8,128]{2,1,0:T(8,128)(2,1)S(1)} %combine.1), channel_id=1, replica_groups=mesh['kvh'=4,'y'=4,'z'=4,'core'=2] {'core','z','y','kvh'}, dimensions={0} | all-to-all | bytes 524288 | tf_op jit(solution)/shard_map/all_to_all | solution.py:284
  36.0 0.0 copy-done
  36.0 0.0 copy-done.1
  36.0 0.0 copy-done.2
  36.0 0.0 slice-start.1
  36.1 0.0 slice-start.3
  36.1 0.0 slice-start.5
  36.1 0.8 %project.1 = (f32[8,128]{1,0:T(8,128)S(1)}, bf16[16,80,128]{2,1,0:T(8,128)(2,1)S(1)}) custom-call(bf16[128,8,128]{2,1,0:T(8,128)(2,1)S(1)} %all_to_all.21.heads, f32[8,128]{1,0:T(8,128)S(1)} %copy-done.1, f32[1,128]{1,0:T(1,128)S(1)} %bitcast.14, bf16[16384,128]{1,0:T(8,128)(2,1)S(1)} %copy-done), custom_call_target="tpu_custom_call" | custom-call | flops 20000000000 | bytes 60000000 | tf_op jit(solution)/shard_map/project/pallas_call | solution.py:220
  36.9 15.5 %all_to_all.22.tiles = bf16[128,5,2,128]{3,2,1,0:T(2,128)(2,1)S(1)} all-to-all(bf16[128,5,2,128]{3,2,1,0:T(2,128)(2,1)S(1)} %bitcast.5), channel_id=1, replica_groups=mesh['kvh'=4,'y'=4,'z'=4,'core'=2] {'core','z','y','kvh'}, dimensions={0} | all-to-all | bytes 655360 | tf_op jit(solution)/shard_map/all_to_all | solution.py:297
  52.4 0.0 slice-done
  52.4 0.0 slice-done.2
  52.4 0.0 slice-done.4
  52.4 0.0 slice-done.1
  52.4 0.0 slice-done.3
  52.4 0.0 slice-done.5
  52.4 3.2 %feed.1 = (bf16[128,8,128]{2,1,0:T(8,128)(2,1)S(1)}, bf16[8,2,128,128]{3,2,1,0:T(8,128)(2,1)}, bf16[8,2,128,128]{3,2,1,0:T(8,128)(2,1)}) custom-call(bf16[128,5,2,128]{3,2,1,0:T(2,128)(2,1)S(1)} %all_to_all.22.tiles, bf16[208,16384]{1,0:T(8,128)(2,1)S(1)} %bitcast.9, bf16[208,16384]{1,0:T(8,128)(2,1)S(1)} %bitcast.11, bf16[208,16384]{1,0:T(8,128)(2,1)S(1)} %bitcast.13, ...), custom_call_target="tpu_custom_call" | custom-call | flops 20000000000 | bytes 60000000 | tf_op jit(solution)/shard_map/feed/pallas_call | solution.py:220
  55.7 14.8 %all_to_all.23.sums = bf16[128,8,128]{2,1,0:T(8,128)(2,1)S(1)} all-to-all(bf16[128,8,128]{2,1,0:T(8,128)(2,1)S(1)} %get-tuple-element.15), channel_id=1, replica_groups=mesh['kvh'=4,'y'=4,'z'=4,'core'=2] {'core','z','y','kvh'}, dimensions={0} | all-to-all | bytes 524288 | tf_op jit(solution)/shard_map/all_to_all | solution.py:311
  70.4 0.6 finish.1
  (3 shorter events, 0.0 us)
Async XLA Ops:
  19.4 16.6 %copy-start = (bf16[16384,128]{1,0:T(8,128)(2,1)S(1)}, bf16[16384,128]{1,0:T(8,128)(2,1)}, u32[]{:S(2)}) copy-start(bf16[16384,128]{1,0:T(8,128)(2,1)} %weight.1) | copy-start | bytes 12582916
  19.4 16.6 %copy-start.1 = (f32[8,128]{1,0:T(8,128)S(1)}, f32[8,128]{1,0:T(8,128)}, u32[]{:S(2)}) copy-start(f32[8,128]{1,0:T(8,128)} %residual.1) | copy-start | bytes 12292
  19.4 16.6 %copy-start.2 = (f32[128]{0:T(128)S(1)}, f32[128]{0:T(128)}, u32[]{:S(2)}) copy-start(f32[128]{0:T(128)} %param.21) | copy-start | bytes 1540
  19.4 33.0 %slice-start = ((s8[6815744]{0:T(1024)(128)(4,1)}), s8[4194304]{0:T(1024)(128)(4,1)S(1)}, s32[]{:S(2)}) async-start(s8[6815744]{0:T(1024)(128)(4,1)} %bitcast.8), calls=%async_computation.4 | async-start | bytes 8388608
  19.4 32.9 %slice-start.2 = ((s8[6815744]{0:T(1024)(128)(4,1)}), s8[4194304]{0:T(1024)(128)(4,1)S(1)}, s32[]{:S(2)}) async-start(s8[6815744]{0:T(1024)(128)(4,1)} %bitcast.10), calls=%async_computation.6 | async-start | bytes 8388608
  19.4 32.9 %slice-start.4 = ((s8[6815744]{0:T(1024)(128)(4,1)}), s8[4194304]{0:T(1024)(128)(4,1)S(1)}, s32[]{:S(2)}) async-start(s8[6815744]{0:T(1024)(128)(4,1)} %bitcast.12), calls=%async_computation.8 | async-start | bytes 8388608
  36.0 16.3 %slice-start.1 = ((s8[6815744]{0:T(1024)(128)(4,1)}), s8[2621440]{0:T(1024)(128)(4,1)S(1)}, s32[]{:S(2)}) async-start(s8[6815744]{0:T(1024)(128)(4,1)} %bitcast.8), calls=%async_computation.5 | async-start | bytes 5242880
  36.1 16.3 %slice-start.3 = ((s8[6815744]{0:T(1024)(128)(4,1)}), s8[2621440]{0:T(1024)(128)(4,1)S(1)}, s32[]{:S(2)}) async-start(s8[6815744]{0:T(1024)(128)(4,1)} %bitcast.10), calls=%async_computation.7 | async-start | bytes 5242880
  36.1 16.3 %slice-start.5 = ((s8[6815744]{0:T(1024)(128)(4,1)}), s8[2621440]{0:T(1024)(128)(4,1)S(1)}, s32[]{:S(2)}) async-start(s8[6815744]{0:T(1024)(128)(4,1)} %bitcast.12), calls=%async_computation.9 | async-start | bytes 5242880

commit v6 on v5

--- a/solution.py
+++ b/solution.py
@@ -13,7 +13,7 @@
 SEQ = ("y", "z", "core")
 EVERY = ("kvh", "y", "z", "core")
 SIZES = (4, 4, 4, 2)
-ORDER = ("core", "z", "y", "kvh")
+ORDER = ("core", "z", "kvh", "y")
 SLOT = np.arange(128).reshape(SIZES).transpose([EVERY.index(axis) for axis in ORDER]).reshape(-1).argsort().tolist()
 VMEM = pl.BlockSpec(memory_space=pltpu.VMEM)
 ANY = pl.BlockSpec(memory_space=pl.ANY)

time: 71.3 us -> 71.1 us (level)
  no operation moved by 1% of the time
where the time goes in v6:
time: 71.1 us; the launch traced here: 70.9 us
  blocking collectives  63.2 us (89%)
  Pallas kernels  6.85 us (10%)
  between operations  0.77 us (1%)
    all_to_all x1, blocking collectives, body(): lax.all_to_all(partials, SEQ, 0, 0)  16.8 us
    all_to_all x1, blocking collectives, body(): all_heads = lax.all_to_all(heads, ORDER, 0, 0)  16.1 us
    all_to_all x1, blocking collectives, body(): all_stream = lax.all_to_all(stream, ORDER, 0, 0)  15.3 us
    all_to_all x1, blocking collectives, body(): all_sums = lax.all_to_all(sums, ORDER, 0, 0)  15 us
    pallas_call x5, Pallas kernels, call(): pl.pallas_call(kernel, out_shape=out_shape, in_specs=in_specs, out_specs=...  6.85 us

profile of v6, /device:TPU:1, one launch (start us, length us, event | category | flops | bytes accessed | tf_op | source)
XLA Modules:
  0.0 70.9 jit_solution(15908321457533765076)
XLA Ops:
  0.6 2.0 %attention.1 = (bf16[320,128]{1,0:T(8,128)(2,1)S(1)}, bf16[8,2,128,128]{3,2,1,0:T(8,128)(2,1)S(1)}, bf16[8,2,128,128]{3,2,1,0:T(8,128)(2,1)S(1)}) custom-call(s32[8]{0:T(128)} %new_block_hbm.1, s32[8]{0:T(128)} %bitcast.15, bf16[8,32,128]{2,1,0:T(8,128)(2,1)} %queries_hbm.1, bf16[8,2,128,128]{3,2,1,0:T(8,128)(2,1)} %keys_hbm.1, ...), custom_call_target="tpu_custom_call" | custom-call | flops 20000000000 | bytes 60000000 | tf_op jit(solution)/shard_map/attention/pallas_call | solution.py:220
  2.6 16.8 %all_to_all.20 = bf16[32,5,2,128]{3,2,1,0:T(2,128)(2,1)S(1)} all-to-all(bf16[32,5,2,128]{3,2,1,0:T(2,128)(2,1)S(1)} %bitcast.6), channel_id=1, replica_groups=mesh['kvh'=4,'y'=4,'z'=4,'core'=2] {'y','z','core'}, dimensions={0} | all-to-all | bytes 163840 | tf_op jit(solution)/shard_map/all_to_all | solution.py:274
  19.4 0.0 copy-start
  19.4 0.0 copy-start.1
  19.4 0.0 copy-start.2
  19.4 0.0 slice-start
  19.4 0.0 slice-start.2
  19.4 0.0 slice-start.4
  19.5 0.2 combine.1
  19.7 16.1 %all_to_all.21.heads = bf16[128,8,128]{2,1,0:T(8,128)(2,1)S(1)} all-to-all(bf16[128,8,128]{2,1,0:T(8,128)(2,1)S(1)} %combine.1), channel_id=1, replica_groups=mesh['kvh'=4,'y'=4,'z'=4,'core'=2] {'core','z','kvh','y'}, dimensions={0} | all-to-all | bytes 524288 | tf_op jit(solution)/shard_map/all_to_all | solution.py:284
  35.8 0.0 copy-done
  35.8 0.0 copy-done.1
  35.8 0.0 copy-done.2
  35.8 0.0 slice-start.1
  35.9 0.0 slice-start.3
  35.9 0.0 slice-start.5
  35.9 0.8 %project.1 = (f32[8,128]{1,0:T(8,128)S(1)}, bf16[16,80,128]{2,1,0:T(8,128)(2,1)S(1)}) custom-call(bf16[128,8,128]{2,1,0:T(8,128)(2,1)S(1)} %all_to_all.21.heads, f32[8,128]{1,0:T(8,128)S(1)} %copy-done.1, f32[1,128]{1,0:T(1,128)S(1)} %bitcast.14, bf16[16384,128]{1,0:T(8,128)(2,1)S(1)} %copy-done), custom_call_target="tpu_custom_call" | custom-call | flops 20000000000 | bytes 60000000 | tf_op jit(solution)/shard_map/project/pallas_call | solution.py:220
  36.7 15.3 %all_to_all.22.tiles = bf16[128,5,2,128]{3,2,1,0:T(2,128)(2,1)S(1)} all-to-all(bf16[128,5,2,128]{3,2,1,0:T(2,128)(2,1)S(1)} %bitcast.5), channel_id=1, replica_groups=mesh['kvh'=4,'y'=4,'z'=4,'core'=2] {'core','z','kvh','y'}, dimensions={0} | all-to-all | bytes 655360 | tf_op jit(solution)/shard_map/all_to_all | solution.py:297
  52.0 0.0 slice-done
  52.0 0.0 slice-done.2
  52.0 0.0 slice-done.4
  52.0 0.0 slice-done.1
  52.0 0.0 slice-done.3
  52.0 0.0 slice-done.5
  52.0 3.2 %feed.1 = (bf16[128,8,128]{2,1,0:T(8,128)(2,1)S(1)}, bf16[8,2,128,128]{3,2,1,0:T(8,128)(2,1)}, bf16[8,2,128,128]{3,2,1,0:T(8,128)(2,1)}) custom-call(bf16[128,5,2,128]{3,2,1,0:T(2,128)(2,1)S(1)} %all_to_all.22.tiles, bf16[208,16384]{1,0:T(8,128)(2,1)S(1)} %bitcast.9, bf16[208,16384]{1,0:T(8,128)(2,1)S(1)} %bitcast.11, bf16[208,16384]{1,0:T(8,128)(2,1)S(1)} %bitcast.13, ...), custom_call_target="tpu_custom_call" | custom-call | flops 20000000000 | bytes 60000000 | tf_op jit(solution)/shard_map/feed/pallas_call | solution.py:220
  55.2 15.0 %all_to_all.23.sums = bf16[128,8,128]{2,1,0:T(8,128)(2,1)S(1)} all-to-all(bf16[128,8,128]{2,1,0:T(8,128)(2,1)S(1)} %get-tuple-element.15), channel_id=1, replica_groups=mesh['kvh'=4,'y'=4,'z'=4,'core'=2] {'core','z','kvh','y'}, dimensions={0} | all-to-all | bytes 524288 | tf_op jit(solution)/shard_map/all_to_all | solution.py:311
  70.2 0.6 finish.1
  (3 shorter events, 0.0 us)
Async XLA Ops:
  19.4 16.4 %copy-start = (bf16[16384,128]{1,0:T(8,128)(2,1)S(1)}, bf16[16384,128]{1,0:T(8,128)(2,1)}, u32[]{:S(2)}) copy-start(bf16[16384,128]{1,0:T(8,128)(2,1)} %weight.1) | copy-start | bytes 12582916
  19.4 16.4 %copy-start.1 = (f32[8,128]{1,0:T(8,128)S(1)}, f32[8,128]{1,0:T(8,128)}, u32[]{:S(2)}) copy-start(f32[8,128]{1,0:T(8,128)} %residual.1) | copy-start | bytes 12292
  19.4 16.4 %copy-start.2 = (f32[128]{0:T(128)S(1)}, f32[128]{0:T(128)}, u32[]{:S(2)}) copy-start(f32[128]{0:T(128)} %param.21) | copy-start | bytes 1540
  19.4 32.5 %slice-start = ((s8[6815744]{0:T(1024)(128)(4,1)}), s8[4194304]{0:T(1024)(128)(4,1)S(1)}, s32[]{:S(2)}) async-start(s8[6815744]{0:T(1024)(128)(4,1)} %bitcast.8), calls=%async_computation.4 | async-start | bytes 8388608
  19.4 32.5 %slice-start.2 = ((s8[6815744]{0:T(1024)(128)(4,1)}), s8[4194304]{0:T(1024)(128)(4,1)S(1)}, s32[]{:S(2)}) async-start(s8[6815744]{0:T(1024)(128)(4,1)} %bitcast.10), calls=%async_computation.6 | async-start | bytes 8388608
  19.4 32.5 %slice-start.4 = ((s8[6815744]{0:T(1024)(128)(4,1)}), s8[4194304]{0:T(1024)(128)(4,1)S(1)}, s32[]{:S(2)}) async-start(s8[6815744]{0:T(1024)(128)(4,1)} %bitcast.12), calls=%async_computation.8 | async-start | bytes 8388608
  35.8 16.1 %slice-start.1 = ((s8[6815744]{0:T(1024)(128)(4,1)}), s8[2621440]{0:T(1024)(128)(4,1)S(1)}, s32[]{:S(2)}) async-start(s8[6815744]{0:T(1024)(128)(4,1)} %bitcast.8), calls=%async_computation.5 | async-start | bytes 5242880
  35.9 16.1 %slice-start.3 = ((s8[6815744]{0:T(1024)(128)(4,1)}), s8[2621440]{0:T(1024)(128)(4,1)S(1)}, s32[]{:S(2)}) async-start(s8[6815744]{0:T(1024)(128)(4,1)} %bitcast.10), calls=%async_computation.7 | async-start | bytes 5242880
  35.9 16.1 %slice-start.5 = ((s8[6815744]{0:T(1024)(128)(4,1)}), s8[2621440]{0:T(1024)(128)(4,1)S(1)}, s32[]{:S(2)}) async-start(s8[6815744]{0:T(1024)(128)(4,1)} %bitcast.12), calls=%async_computation.9 | async-start | bytes 5242880
